TPU v7x, 32 devices: a whole 2x2x4 slice. The times are simulated.
32 devices in a mesh: groups: 2 (over x), seq: 16 (over z, y, core).
Axes of the slice: x: 2, y: 2, z: 4, core: 2. Of those that a mesh axis runs over, the one named last changes fastest.
Arguments:
- qkv: bfloat16 [4096, 9216], P(('groups', 'seq')), parts along dimension 0, may hold values from -8 to 8, as said below
- output_gradient: bfloat16 [4096, 3072], P(('groups', 'seq')), parts along dimension 0, may hold values from -6 to 6
- adapter_down_weight: bfloat16 [3072, 64], replicated, may hold values from -0.109375 to 0.109375
- adapter_up_weight: bfloat16 [64, 3072], replicated, may hold values from -0.75 to 0.75
- listed_key_blocks: int32 [48, 16, 10], replicated, may hold values from 0 to 15
- key_block_count: int32 [48], replicated, may hold values from 1 to 10
Outputs:
- grad_qkv: bfloat16 [4096, 9216], P(('groups', 'seq')), parts along dimension 0
- grad_down: float32 [6144, 64], P('groups'), parts along dimension 0
- grad_up: float32 [128, 3072], P('groups'), parts along dimension 0
There are 2 independent parts, one for each index of `groups`. A program takes and returns all parts, laid end to end along the dimension named above; an argument that names none is the same for every part. Nothing has to cross between parts.
Inputs may be any that keep to these rules, and one draw needn't show every extreme that they name: `qkv`: query, key and value entries.
All inputs are finite; a program needn't handle non-finite values.
Results may differ from a plain program's by a relative error of at most 0.019.
Values may be sent and summed in bfloat16 or wider, within the bound.
A program may use at most 192 MiB of HBM per device.

v0:
```python
import jax
import jax.numpy as jnp
import numpy as np
from jax import lax
from jax.sharding import PartitionSpec as P

H = 48
E = 64
BLOCK = 128
KB = 10
ITEMS_DEV = 3


def tables(device_total, segments):
    slot_total = -(-ITEMS_DEV // segments)
    head_slots = min(ITEMS_DEV, (ITEMS_DEV + segments - 2) // segments + 1)
    device = np.repeat(np.arange(device_total), ITEMS_DEV)
    within = np.tile(np.arange(ITEMS_DEV), device_total)
    item_id = device * ITEMS_DEV + within
    head_for = np.full((segments, device_total, slot_total), H, np.int32)
    head_for[item_id % segments, device, within // segments] = item_id // segments
    source_for = np.zeros((segments, H), np.int32)
    source_for[item_id % segments, item_id // segments] = within // segments * device_total + device
    item_heads = (item_id // segments).reshape(device_total, ITEMS_DEV).astype(np.int32)
    first_head = np.arange(device_total) * ITEMS_DEV // segments
    last_head = (np.arange(device_total) * ITEMS_DEV + ITEMS_DEV - 1) // segments
    slot_heads = np.minimum(
        first_head[:, None] + np.arange(head_slots)[None, :], last_head[:, None]
    ).astype(np.int32)
    owned_heads = []
    owned_rows = []
    for slot_pos in range(head_slots):
        usable = first_head + slot_pos <= last_head
        owned_heads.append((first_head + slot_pos)[usable])
        owned_rows.append((slot_pos * device_total + np.arange(device_total))[usable])
    owned_heads = np.concatenate(owned_heads)
    owned_rows = np.concatenate(owned_rows)
    ordering = np.argsort(owned_heads, kind="stable")
    sorted_heads = owned_heads[ordering]
    sorted_rows = owned_rows[ordering]
    position = np.arange(sorted_heads.size) - np.searchsorted(sorted_heads, sorted_heads)
    contributors = np.full((H, int(position.max()) + 1), head_slots * device_total, np.int32)
    contributors[sorted_heads, position] = sorted_rows
    return (head_for, source_for, item_heads, slot_heads, contributors)


def spread_rows(features, targets):
    shard_rows = features.shape[0]
    per_head = jnp.transpose(features.reshape(shard_rows, H, E), (1, 0, 2))
    padded = jnp.concatenate([per_head, jnp.zeros((1, shard_rows, E), features.dtype)], axis=0)
    return jnp.take(padded, targets, axis=0).reshape(targets.shape[0], -1)


def collect_heads(received, sources, shard_rows):
    flattened = received.reshape(-1, shard_rows * E)
    picked = jnp.take(flattened, sources, axis=0)
    return jnp.transpose(picked.reshape(H, shard_rows, E), (1, 0, 2)).reshape(shard_rows, H * E)


def place_items(pieces, segment_ids, slot_total, segments):
    per_source = pieces[0].shape[0]
    buffer = jnp.zeros((slot_total, per_source, segments, pieces[0][0].size), jnp.bfloat16)
    anchor = jnp.zeros((), jnp.int32)
    for within in range(len(pieces)):
        update = pieces[within].reshape(1, per_source, 1, -1)
        slot_start = jnp.full((), within // segments, jnp.int32)
        buffer = lax.dynamic_update_slice(
            buffer, update, (slot_start, anchor, segment_ids[within], anchor)
        )
    return buffer.reshape(slot_total, per_source * segments, -1)


def shards(
    qkv, output_gradient, adapter_down_weight, adapter_up_weight, listed_key_blocks, key_block_count
):
    device_total = lax.axis_size("seq")
    my_index = lax.axis_index("seq")
    shard_rows = qkv.shape[0]
    segments = ITEMS_DEV * device_total // H
    slot_total = -(-ITEMS_DEV // segments)
    per_source = device_total // segments
    blocks_per_shard = shard_rows // BLOCK
    block_total = device_total * blocks_per_shard
    head_for, source_for, item_heads, slot_heads, contributors = tables(device_total, segments)
    head_slots = slot_heads.shape[1]
    residue = my_index % segments
    targets = lax.dynamic_index_in_dim(jnp.asarray(head_for), residue, 0, False)
    sources = lax.dynamic_index_in_dim(jnp.asarray(source_for), residue, 0, False)
    query_send = spread_rows(qkv[:, : H * E], targets)
    key_part = qkv[:, H * E : 2 * H * E].reshape(shard_rows, H, E)
    value_part = qkv[:, 2 * H * E :].reshape(shard_rows, H, E)
    keyval_heads = jnp.transpose(
        jnp.concatenate([key_part, value_part], axis=2), (1, 0, 2)
    ).reshape(H, shard_rows * 2 * E)
    first_head = my_index * ITEMS_DEV // segments
    received_queries, received_keyval = (
        lax.all_to_all(query_send, "seq", split_axis=0, concat_axis=0, tiled=True),
        lax.all_to_all(
            jnp.take(keyval_heads, jnp.asarray(item_heads), axis=0),
            "seq",
            split_axis=0,
            concat_axis=0,
            tiled=True,
        ),
    )
    queries_by_source = received_queries.reshape(per_source, segments, slot_total, shard_rows, E)
    keyval_by_slot = received_keyval.reshape(device_total, -1, shard_rows * 2 * E)
    source_ids = jnp.arange(per_source, dtype=jnp.int32)
    column_block = jnp.arange(KB * BLOCK, dtype=jnp.int32) // BLOCK
    saved = []
    for within in range(ITEMS_DEV):
        item_id = my_index * ITEMS_DEV + within
        item_head = item_id // segments
        segment = item_id % segments
        queries = lax.dynamic_index_in_dim(queries_by_source, segment, 1, False)[
            :, within // segments
        ]
        query_ids = (
            (segment + segments * source_ids)[:, None] * blocks_per_shard
            + jnp.arange(blocks_per_shard, dtype=jnp.int32)[None, :]
        ).reshape(-1)
        item_blocks = jnp.take(
            lax.dynamic_index_in_dim(listed_key_blocks, item_head, 0, False), query_ids, axis=0
        )
        keyval_item = lax.dynamic_index_in_dim(keyval_by_slot, within, 1, False).reshape(
            block_total, BLOCK, 2 * E
        )
        gathered = jnp.take(keyval_item, item_blocks, axis=0).reshape(-1, KB * BLOCK, 2 * E)
        live_cols = column_block < key_block_count[item_head]
        raw_scores = jnp.einsum(
            "qre,qke->qrk", queries, gathered[..., :E], preferred_element_type=jnp.float32
        ) * E ** (-0.5)
        scores = jnp.where(live_cols, raw_scores, -jnp.inf)
        row_peak = jnp.max(scores, axis=-1, keepdims=True)
        log_total = row_peak + jnp.log(jnp.sum(jnp.exp(scores - row_peak), axis=-1, keepdims=True))
        weights = jnp.exp(scores - log_total).astype(jnp.bfloat16)
        attention_output = jnp.einsum(
            "qrk,qke->qre", weights, gathered[..., E:], preferred_element_type=jnp.float32
        ).astype(jnp.bfloat16)
        saved.append(
            (item_head, segment, queries, gathered, item_blocks, weights, attention_output)
        )
    segment_ids = [entry[1] for entry in saved]
    attended_send = place_items([entry[6] for entry in saved], segment_ids, slot_total, segments)
    attended_back = lax.all_to_all(attended_send, "seq", split_axis=1, concat_axis=1, tiled=True)
    attention_output_rows = collect_heads(attended_back, sources, shard_rows)
    adapter_projected = jnp.dot(
        attention_output_rows, adapter_down_weight, preferred_element_type=jnp.float32
    ).astype(jnp.bfloat16)
    fetched_rows = jnp.einsum(
        "ec,sc->es", output_gradient, adapter_up_weight, preferred_element_type=jnp.float32
    ).astype(jnp.bfloat16)
    attention_output_gradient = (
        output_gradient.astype(jnp.float32)
        + jnp.einsum(
            "ab,eb->ae", fetched_rows, adapter_down_weight, preferred_element_type=jnp.float32
        )
    ).astype(jnp.bfloat16)
    cotangent_in = lax.all_to_all(
        spread_rows(attention_output_gradient, targets),
        "seq",
        split_axis=0,
        concat_axis=0,
        tiled=True,
    )
    down_term = jnp.einsum(
        "td,tr->dr", attention_output_rows, fetched_rows, preferred_element_type=jnp.float32
    )
    up_term = jnp.einsum(
        "tr,td->rd", adapter_projected, output_gradient, preferred_element_type=jnp.float32
    )
    grad_down, grad_up = lax.psum((down_term, up_term), "seq")
    rescale = (shard_rows * device_total) ** (-0.5)
    cotangent_by_source = cotangent_in.reshape(per_source, segments, slot_total, shard_rows, E)
    key_sums = jnp.zeros((head_slots, block_total, BLOCK, E), jnp.float32)
    value_sums = jnp.zeros((head_slots, block_total, BLOCK, E), jnp.float32)
    query_pieces = []
    for within in range(ITEMS_DEV):
        item_head, segment, queries, gathered, item_blocks, weights, attention_output = saved[
            within
        ]
        grad_item = lax.dynamic_index_in_dim(cotangent_by_source, segment, 1, False)[
            :, within // segments
        ]
        value_grad = jnp.einsum(
            "qrk,qre->qke", weights, grad_item, preferred_element_type=jnp.float32
        )
        dotted = jnp.einsum(
            "qre,qke->qrk", grad_item, gathered[..., E:], preferred_element_type=jnp.float32
        ).astype(jnp.bfloat16)
        row_delta = jnp.sum(
            grad_item.astype(jnp.float32) * attention_output.astype(jnp.float32),
            axis=-1,
            keepdims=True,
        )
        score_grad = (
            weights.astype(jnp.float32) * (dotted.astype(jnp.float32) - row_delta)
        ).astype(jnp.bfloat16)
        query_grad = (
            jnp.einsum(
                "qrk,qke->qre", score_grad, gathered[..., :E], preferred_element_type=jnp.float32
            )
            * E ** (-0.5)
        ).astype(jnp.bfloat16)
        key_grad = jnp.einsum(
            "qrk,qre->qke", score_grad, queries, preferred_element_type=jnp.float32
        ) * E ** (-0.5)
        slot_now = item_head - first_head
        key_sums = key_sums.at[slot_now, item_blocks].add(key_grad.reshape(-1, KB, BLOCK, E))
        value_sums = value_sums.at[slot_now, item_blocks].add(value_grad.reshape(-1, KB, BLOCK, E))
        query_pieces.append(query_grad)
    query_send_back = place_items(query_pieces, segment_ids, slot_total, segments)
    keyval_send_back = (
        jnp.concatenate([key_sums, value_sums], axis=-1)
        .astype(jnp.bfloat16)
        .reshape(head_slots, device_total, shard_rows * 2 * E)
    )
    query_back, keyval_back = (
        lax.all_to_all(query_send_back, "seq", split_axis=1, concat_axis=1, tiled=True),
        lax.all_to_all(keyval_send_back, "seq", split_axis=1, concat_axis=1, tiled=True),
    )
    query_rows = collect_heads(query_back, sources, shard_rows)
    stacked = jnp.concatenate(
        [
            keyval_back.reshape(head_slots * device_total, shard_rows * 2 * E),
            jnp.zeros((1, shard_rows * 2 * E), jnp.bfloat16),
        ],
        axis=0,
    )
    summed = jnp.sum(
        jnp.take(stacked, jnp.asarray(contributors), axis=0), axis=1, dtype=jnp.float32
    ).astype(jnp.bfloat16)
    keyval_rows = jnp.transpose(summed.reshape(H, shard_rows, 2 * E), (1, 0, 2))
    key_rows = keyval_rows[..., :E].reshape(shard_rows, H * E)
    value_rows = keyval_rows[..., E:].reshape(shard_rows, H * E)
    grad_qkv = jnp.concatenate([query_rows, key_rows, value_rows], axis=1)
    return (grad_qkv, grad_down * rescale, grad_up * rescale)


def solution(mesh):
    return jax.shard_map(
        shards,
        mesh=mesh,
        in_specs=(P(("groups", "seq"), None), P(("groups", "seq"), None), P(), P(), P(), P()),
        out_specs=(P(("groups", "seq"), None), P("groups", None), P("groups", None)),
        check_vma=False,
    )
```

profile of v0, /device:TPU:0, one launch (start us, length us, event | category | flops | bytes accessed | tf_op | source)
XLA Modules:
  0.0 707.4 jit_solution(2381334462430455134)
XLA Ops:
  17.8 5.5 reduce.8
  24.7 7.6 %all-to-all-start = ((bf16[16,2,12288]{2,1,0:T(2,128)(2,1)}), bf16[16,2,12288]{2,1,0:T(2,128)(2,1)}, u32[]{:S(2)}, u32[]{:S(2)}) async-start(bf16[16,2,12288]{2,1,0:T(2,128)(2,1)} %reshape.445), calls=%async_computation | async-start | bytes 1572864 | tf_op jit(solution)/shard_map/all_to_all | solution.py:97
  37.7 6.5 reduce.9
  51.1 5.5 all-to-all-start.2
  64.9 10.6 %all-to-all-done.2 = bf16[16,2,12288]{2,1,0:T(2,128)(2,1)} async-done(((bf16[16,2,12288]{2,1,0:T(2,128)(2,1)}), bf16[16,2,12288]{2,1,0:T(2,128)(2,1)}, u32[]{:S(2)}, u32[]{:S(2)}) %all-to-all-start.2) | async-done | bytes 786464 | tf_op jit(solution)/shard_map/all_to_all | solution.py:159
  75.4 5.8 all-to-all-start.1
  106.8 5.6 reduce.2
  122.3 10.2 %slice_reduce_fusion = (bf16[16,16384]{1,0:T(8,128)(2,1)S(1)}, bf16[16,16384]{1,0:T(8,128)(2,1)S(1)}, bf16[16,16384]{1,0:T(8,128)(2,1)S(1)}) fusion(bf16[16,3,16384]{2,1,0:T(4,128)(2,1)} %all-to-all-done.1), kind=kLoop, calls=%fused_computation.81 | loop fusion | bytes 3145728 | tf_op jit(solution)/shard_map/jit(dynamic_index_in_dim)/dynamic_slice | solution.py:125
  132.7 8.0 %gather_fusion.7 = bf16[160,128,128]{2,1,0:T(8,128)(2,1)} fusion(bf16[16,128,128]{2,1,0:T(8,128)(2,1)S(1)} %bitcast.164, s32[1024]{0:T(1024)} %pad_clamp_fusion.5), kind=kCustom, calls=%fused_computation.7.clone | custom fusion | bytes 10486400 | tf_op jit(solution)/shard_map/jit(_take)/gather | solution.py:128
  140.7 7.7 %gather_fusion.9 = bf16[160,128,128]{2,1,0:T(8,128)(2,1)} fusion(bf16[16,128,128]{2,1,0:T(8,128)(2,1)S(1)} %bitcast.163, s32[1024]{0:T(1024)S(1)} %pad_clamp_fusion.4), kind=kCustom, calls=%fused_computation.8.clone | custom fusion | bytes 10486400 | tf_op jit(solution)/shard_map/jit(_take)/gather | solution.py:128
  148.4 6.9 broadcast_select_fusion
  164.9 9.0 %multiply_reduce_fusion.1 = (f32[16,128]{1,0:T(8,128)}, bf16[16,128,64]{1,2,0:T(8,128)(2,1)S(1)}) fusion(bf16[16,1,128,64]{2,3,0,1:T(8,128)(2,1)} %copy.130, bf16[16,128,1280]{2,1,0:T(8,128)(2,1)} %exponential_convert_fusion.1, bf16[16,1280,128]{2,1,0:T(8,128)(2,1)} %bitcast.171), kind=kOutput, calls=%fused_computation.99 | convolution fusion | flops 336197632 | bytes 11018240 | tf_op jit(solution)/shard_map/qrk,qke->qre/dot_general | solution.py:137
  175.5 7.7 %gather_fusion.4 = bf16[160,128,128]{2,1,0:T(8,128)(2,1)} fusion(bf16[16,128,128]{2,1,0:T(8,128)(2,1)S(1)} %bitcast.165, s32[1024]{0:T(1024)S(1)} %pad_clamp_fusion.6), kind=kCustom, calls=%fused_computation.2.clone | custom fusion | bytes 10486400 | tf_op jit(solution)/shard_map/jit(_take)/gather | solution.py:128
  196.3 9.0 %multiply_reduce_fusion.2 = (f32[16,128]{1,0:T(8,128)}, bf16[16,128,64]{1,2,0:T(8,128)(2,1)S(1)}) fusion(bf16[16,1,128,64]{2,3,0,1:T(8,128)(2,1)S(1)} %copy-done.17, bf16[16,128,1280]{2,1,0:T(8,128)(2,1)} %exponential_convert_fusion.2, bf16[16,1280,128]{2,1,0:T(8,128)(2,1)} %bitcast.181), kind=kOutput, calls=%fused_computation.100 | convolution fusion | flops 336197632 | bytes 11018240 | tf_op jit(solution)/shard_map/qrk,qke->qre/dot_general | solution.py:137
  217.8 9.8 %multiply_reduce_fusion = (f32[16,128]{1,0:T(8,128)}, bf16[16,128,64]{1,2,0:T(8,128)(2,1)}) fusion(bf16[16,1,128,64]{2,3,0,1:T(8,128)(2,1)S(1)} %copy-done.16, bf16[16,128,1280]{2,1,0:T(8,128)(2,1)} %exponential_convert_fusion, bf16[16,1280,128]{2,1,0:T(8,128)(2,1)} %bitcast.177), kind=kOutput, calls=%fused_computation.98 | convolution fusion | flops 336197632 | bytes 11018240 | tf_op jit(solution)/shard_map/qrk,qke->qre/dot_general | solution.py:137
  232.7 11.5 %all-to-all-start.5 = ((bf16[3,16,8192]{2,0,1:T(4,128)(2,1)}), bf16[3,16,8192]{2,0,1:T(4,128)(2,1)}, u32[]{:S(2)}, u32[]{:S(2)}) async-start(bf16[3,16,8192]{2,0,1:T(4,128)(2,1)} %copy.115), calls=%async_computation.5 | async-start | bytes 2097152 | tf_op jit(solution)/shard_map/all_to_all | solution.py:145
  244.1 7.6 %multiply_convert_fusion = bf16[16,128,1280]{2,1,0:T(8,128)(2,1)S(1)} fusion(bf16[16,128,1280]{2,1,0:T(8,128)(2,1)} %exponential_convert_fusion, f32[16,128]{1,0:T(8,128)} %get-tuple-element.56, bf16[16,1280,128]{2,1,0:T(8,128)(2,1)} %bitcast.178, bf16[16,3,128,64]{3,2,1,0:T(8,128)(2,1)S(1)} %squeeze.65), kind=kOutput, calls=%fused_computation.18 | convolution fusion | flops 351272960 | bytes 16261120 | tf_op jit(solution)/shard_map/qre,qke->qrk/dot_general | solution.py:188
  254.0 5.2 fusion.43
  261.7 8.1 %multiply_convert_fusion.1 = bf16[16,128,1280]{2,1,0:T(8,128)(2,1)S(1)} fusion(bf16[16,128,1280]{2,1,0:T(8,128)(2,1)} %exponential_convert_fusion.1, f32[16,128]{1,0:T(8,128)} %get-tuple-element.54, bf16[16,1280,128]{2,1,0:T(8,128)(2,1)} %bitcast.172, bf16[16,3,128,64]{3,2,1,0:T(8,128)(2,1)S(1)} %squeeze.65), kind=kOutput, calls=%fused_computation.22 | convolution fusion | flops 351272960 | bytes 16261120 | tf_op jit(solution)/shard_map/qre,qke->qrk/dot_general | solution.py:188
  274.8 8.0 %multiply_convert_fusion.2 = bf16[16,128,1280]{2,1,0:T(8,128)(2,1)S(1)} fusion(bf16[16,128,1280]{2,1,0:T(8,128)(2,1)} %exponential_convert_fusion.2, f32[16,128]{1,0:T(8,128)S(1)} %copy-done.23, bf16[16,1280,128]{2,1,0:T(8,128)(2,1)} %bitcast.182, bf16[16,3,128,64]{3,2,1,0:T(8,128)(2,1)S(1)} %squeeze.65), kind=kOutput, calls=%fused_computation.26 | convolution fusion | flops 351272960 | bytes 16261120 | tf_op jit(solution)/shard_map/qre,qke->qrk/dot_general | solution.py:188
  295.8 5.3 copy.100
  301.1 6.5 reshape.370
  307.7 7.9 %copy.101 = f32[160,128,64]{1,2,0:T(8,128)} copy(f32[160,128,64]{1,0,2:T(8,128)} %reshape.370) | data formatting | bytes 10485760 | tf_op jit(solution)/shard_map/reshape | solution.py:209
  317.6 5.4 copy.98
  323.0 6.7 reshape.364
  329.8 8.1 %copy.99 = f32[160,128,64]{1,2,0:T(8,128)} copy(f32[160,128,64]{1,0,2:T(8,128)} %reshape.364) | data formatting | bytes 10485760 | tf_op jit(solution)/shard_map/reshape | solution.py:209
  339.8 5.3 copy.96
  345.1 6.6 reshape.358
  351.7 7.8 %copy.97 = f32[160,128,64]{1,2,0:T(8,128)} copy(f32[160,128,64]{1,0,2:T(8,128)} %reshape.358) | data formatting | bytes 10485760 | tf_op jit(solution)/shard_map/reshape | solution.py:209
  359.7 18.1 %scatter_fusion = f32[3,16,128,64]{2,3,1,0:T(8,128)S(1)} fusion(f32[3,16,128,64]{2,3,1,0:T(8,128)S(1)} %broadcast.100.clone.1, s32[160]{0:T(256)S(1)} %reshape.356, f32[160,128,64]{1,2,0:T(8,128)} %copy.97), kind=kCustom, calls=%fused_computation.12 | custom fusion | flops 1310720 | bytes 15729920 | tf_op jit(solution)/shard_map/scatter-add | solution.py:209
  377.9 18.1 %scatter_fusion.1 = f32[3,16,128,64]{2,3,1,0:T(8,128)S(1)} fusion(f32[3,16,128,64]{2,3,1,0:T(8,128)S(1)} %scatter_fusion, s32[160]{0:T(256)S(1)} %reshape.362, f32[160,128,64]{1,2,0:T(8,128)} %copy.99), kind=kCustom, calls=%fused_computation.13 | custom fusion | flops 1310720 | bytes 15729920 | tf_op jit(solution)/shard_map/scatter-add | solution.py:209
  396.0 18.1 %scatter_fusion.2 = f32[3,16,128,64]{2,3,1,0:T(8,128)S(1)} fusion(f32[3,16,128,64]{2,3,1,0:T(8,128)S(1)} %scatter_fusion.1, s32[160]{0:T(256)S(1)} %copy-done.1, f32[160,128,64]{1,2,0:T(8,128)} %copy.101), kind=kCustom, calls=%fused_computation.14 | custom fusion | flops 1310720 | bytes 15729920 | tf_op jit(solution)/shard_map/scatter-add | solution.py:209
  415.1 6.6 all-to-all-start.3
  425.2 5.4 copy.106
  430.6 6.6 reshape.388
  437.2 8.0 %copy.107 = f32[160,128,64]{1,2,0:T(8,128)} copy(f32[160,128,64]{1,0,2:T(8,128)} %reshape.388) | data formatting | bytes 10485760 | tf_op jit(solution)/shard_map/reshape | solution.py:210
  446.2 5.3 copy.104
  451.6 6.7 reshape.382
  458.3 8.0 %copy.105 = f32[160,128,64]{1,2,0:T(8,128)} copy(f32[160,128,64]{1,0,2:T(8,128)} %reshape.382) | data formatting | bytes 10485760 | tf_op jit(solution)/shard_map/reshape | solution.py:210
  467.2 5.3 copy.102
  472.5 6.5 reshape.376
  479.0 7.8 %copy.103 = f32[160,128,64]{1,2,0:T(8,128)} copy(f32[160,128,64]{1,0,2:T(8,128)} %reshape.376) | data formatting | bytes 10485760 | tf_op jit(solution)/shard_map/reshape | solution.py:210
  487.0 18.1 %scatter_fusion.3 = f32[3,16,128,64]{2,3,1,0:T(8,128)S(1)} fusion(f32[3,16,128,64]{2,3,1,0:T(8,128)S(1)} %broadcast.100.clone, s32[160]{0:T(256)S(1)} %reshape.356, f32[160,128,64]{1,2,0:T(8,128)} %copy.103), kind=kCustom, calls=%fused_computation.15 | custom fusion | flops 1310720 | bytes 15729920 | tf_op jit(solution)/shard_map/scatter-add | solution.py:210
  505.1 18.3 %scatter_fusion.4 = f32[3,16,128,64]{2,3,1,0:T(8,128)S(1)} fusion(f32[3,16,128,64]{2,3,1,0:T(8,128)S(1)} %scatter_fusion.3, s32[160]{0:T(256)S(1)} %reshape.362, f32[160,128,64]{1,2,0:T(8,128)} %copy.105), kind=kCustom, calls=%fused_computation.16 | custom fusion | flops 1310720 | bytes 15729920 | tf_op jit(solution)/shard_map/scatter-add | solution.py:210
  523.5 18.1 %scatter_fusion.5 = f32[3,16,128,64]{2,3,1,0:T(8,128)S(1)} fusion(f32[3,16,128,64]{2,3,1,0:T(8,128)S(1)} %scatter_fusion.4, s32[160]{0:T(256)S(1)} %copy-done.1, f32[160,128,64]{1,2,0:T(8,128)} %copy.107), kind=kCustom, calls=%fused_computation.17 | custom fusion | flops 1310720 | bytes 15729920 | tf_op jit(solution)/shard_map/scatter-add | solution.py:210
  544.8 6.1 all-to-all-start.4
  575.3 101.4 %all-reduce.11.cloned.1.call-done = (f32[3072,64]{0,1:T(8,128)}, f32[64,3072]{1,0:T(8,128)}) async-done(((f32[3072,64]{0,1:T(8,128)}, f32[64,3072]{1,0:T(8,128)}), (f32[3072,64]{0,1:T(8,128)}, f32[64,3072]{1,0:T(8,128)})) %all-reduce.11.cloned.1.call-update) | async-done | bytes 1572880 | tf_op jit(solution)/shard_map/psum | solution.py:172
  687.7 10.2 %pad_maximum_fusion = bf16[128,9216]{0,1:T(8,128)(2,1)S(1)} fusion(bf16[128,3072]{0,1:T(8,128)(2,1)S(1)} %bitcast.204, bf16[128,3072]{0,1:T(8,128)(2,1)S(1)} %bitcast.203, bf16[128,3072]{0,1:T(8,128)(2,1)} %bitcast.202), kind=kLoop, calls=%fused_computation.65 | loop fusion | flops 7077888 | bytes 4718592 | tf_op jit(solution)/shard_map/concatenate | solution.py:236
  (221 shorter events, 183.7 us)
Async XLA Ops:
  7.2 27.2 %copy-start = (bf16[3072,64]{0,1:T(8,128)(2,1)S(1)}, bf16[3072,64]{0,1:T(8,128)(2,1)}, u32[]{:S(2)}) copy-start(bf16[3072,64]{0,1:T(8,128)(2,1)} %param.20) | copy-start | bytes 1179652
  11.3 21.1 %copy-start.7 = (bf16[128,3072]{1,0:T(8,128)(2,1)S(1)}, bf16[128,3072]{1,0:T(8,128)(2,1)}, u32[]{:S(2)}) copy-start(bf16[128,3072]{1,0:T(8,128)(2,1)} %param.19) | copy-start | bytes 2359300
  24.7 26.4 %all-to-all-start = ((bf16[16,2,12288]{2,1,0:T(2,128)(2,1)}), bf16[16,2,12288]{2,1,0:T(2,128)(2,1)}, u32[]{:S(2)}, u32[]{:S(2)}) async-start(bf16[16,2,12288]{2,1,0:T(2,128)(2,1)} %reshape.445), calls=%async_computation | async-start | bytes 1572864 | tf_op jit(solution)/shard_map/all_to_all | solution.py:97
  33.8 0.6 copy-start.18
  37.6 19.0 %copy-start.10 = (bf16[128,3072]{1,0:T(8,128)(2,1)S(1)}, bf16[128,3072]{1,0:T(8,128)(2,1)}, u32[]{:S(2)}) copy-start(bf16[128,3072]{1,0:T(8,128)(2,1)} %get-tuple-element.25) | copy-start | bytes 2359300
  37.7 20.1 %copy-start.9 = (bf16[128,3072]{1,0:T(8,128)(2,1)S(1)}, bf16[128,3072]{1,0:T(8,128)(2,1)}, u32[]{:S(2)}) copy-start(bf16[128,3072]{1,0:T(8,128)(2,1)} %get-tuple-element.26) | copy-start | bytes 2359300
  51.1 24.3 %all-to-all-start.2 = ((bf16[16,2,12288]{2,1,0:T(2,128)(2,1)}), bf16[16,2,12288]{2,1,0:T(2,128)(2,1)}, u32[]{:S(2)}, u32[]{:S(2)}) async-start(bf16[16,2,12288]{2,1,0:T(2,128)(2,1)} %reshape.447), calls=%async_computation.2 | async-start | bytes 1572864 | tf_op jit(solution)/shard_map/all_to_all | solution.py:159
  62.9 18.2 %copy-start.15 = (s32[48,16,10]{0,1,2:T(8,128)S(1)}, s32[48,16,10]{0,1,2:T(8,128)}, u32[]{:S(2)}) copy-start(s32[48,16,10]{0,1,2:T(8,128)} %param.22) | copy-start | bytes 92164
  63.0 22.5 %copy-start.27 = (s32[48]{0:T(128)S(1)}, s32[48]{0:T(128)}, u32[]{:S(2)}) copy-start(s32[48]{0:T(128)} %param.23) | copy-start | bytes 580
  75.4 46.9 %all-to-all-start.1 = ((bf16[16,3,16384]{2,1,0:T(4,128)(2,1)}), bf16[16,3,16384]{2,1,0:T(4,128)(2,1)}, u32[]{:S(2)}, u32[]{:S(2)}) async-start(bf16[16,3,16384]{2,1,0:T(4,128)(2,1)} %reshape.341), calls=%async_computation.1 | async-start | bytes 4194304 | tf_op jit(solution)/shard_map/all_to_all | solution.py:98
  140.7 7.7 %copy-start.24 = (pred[16,10]{1,0:T(8,128)(4,1)S(1)}, pred[16,10]{1,0:T(8,128)(4,1)}, u32[]{:S(2)}) copy-start(pred[16,10]{1,0:T(8,128)(4,1)} %get-tuple-element.18) | copy-start | bytes 484
  140.7 7.7 %copy-start.25 = (pred[16,10]{1,0:T(8,128)(4,1)S(1)}, pred[16,10]{1,0:T(8,128)(4,1)}, u32[]{:S(2)}) copy-start(pred[16,10]{1,0:T(8,128)(4,1)} %get-tuple-element.40) | copy-start | bytes 484
  148.4 6.9 copy-start.22
  155.4 3.0 copy-start.2
  175.5 7.8 %copy-start.26 = (pred[16,10]{1,0:T(8,128)(4,1)S(1)}, pred[16,10]{1,0:T(8,128)(4,1)}, u32[]{:S(2)}) copy-start(pred[16,10]{1,0:T(8,128)(4,1)} %get-tuple-element.42) | copy-start | bytes 484
  183.2 3.0 copy-start.21
  186.3 3.5 copy-start.3
  192.0 4.3 copy-start.17
  196.3 10.7 %copy-start.20 = (pred[1280]{0:T(1024)(128)(4,1)S(1)}, pred[1280]{0:T(1024)(128)(4,1)}, u32[]{:S(2)}) copy-start(pred[1280]{0:T(1024)(128)(4,1)} %fusion.69) | copy-start | bytes 3844
  213.5 4.3 copy-start.16
  217.8 12.2 %copy-start.11 = (bf16[3,16,8192]{2,1,0:T(8,128)(2,1)S(1)}, bf16[3,16,8192]{2,1,0:T(8,128)(2,1)}, u32[]{:S(2)}) copy-start(bf16[3,16,8192]{2,1,0:T(8,128)(2,1)} %pad_bitcast_fusion) | copy-start | bytes 2359300
  217.8 12.2 %copy-start.13 = (bf16[1,16,8192]{2,1,0:T(8,128)(2,1)S(1)}, bf16[1,16,8192]{2,1,0:T(8,128)(2,1)}, u32[]{:S(2)}) copy-start(bf16[1,16,8192]{2,1,0:T(8,128)(2,1)} %reshape.255) | copy-start | bytes 786436
  232.7 182.5 %all-to-all-start.5 = ((bf16[3,16,8192]{2,0,1:T(4,128)(2,1)}), bf16[3,16,8192]{2,0,1:T(4,128)(2,1)}, u32[]{:S(2)}, u32[]{:S(2)}) async-start(bf16[3,16,8192]{2,0,1:T(4,128)(2,1)} %copy.115), calls=%async_computation.5 | async-start | bytes 2097152 | tf_op jit(solution)/shard_map/all_to_all | solution.py:145
  251.8 2.3 copy-start.4
  254.0 18.1 %slice-start.4 = ((s8[5242880]{0:T(1024)(128)(4,1)}), s8[1048576]{0:T(1024)(128)(4,1)S(1)}, s32[]{:S(2)}) async-start(s8[5242880]{0:T(1024)(128)(4,1)} %bitcast.173), calls=%async_computation.11 | async-start | bytes 2097152
  261.7 10.4 %slice-start.5 = ((s8[5242880]{0:T(1024)(128)(4,1)}), s8[4194304]{0:T(1024)(128)(4,1)S(1)}, s32[]{:S(2)}) async-start(s8[5242880]{0:T(1024)(128)(4,1)} %bitcast.173), calls=%async_computation.12 | async-start | bytes 8388608
  269.8 2.3 copy-start.5
  272.1 2.7 copy-start.23
  282.9 2.3 copy-start.6
  285.2 5.3 copy-start.14
  301.1 14.5 %slice-start.6 = ((s8[5242880]{0:T(1024)(128)(4,1)}), s8[1048576]{0:T(1024)(128)(4,1)S(1)}, s32[]{:S(2)}) async-start(s8[5242880]{0:T(1024)(128)(4,1)} %bitcast.184), calls=%async_computation.13 | async-start | bytes 2097152
  307.7 7.9 %slice-start.7 = ((s8[5242880]{0:T(1024)(128)(4,1)}), s8[4194304]{0:T(1024)(128)(4,1)S(1)}, s32[]{:S(2)}) async-start(s8[5242880]{0:T(1024)(128)(4,1)} %bitcast.184), calls=%async_computation.14 | async-start | bytes 8388608
  323.0 14.8 %slice-start.8 = ((s8[5242880]{0:T(1024)(128)(4,1)}), s8[1048576]{0:T(1024)(128)(4,1)S(1)}, s32[]{:S(2)}) async-start(s8[5242880]{0:T(1024)(128)(4,1)} %bitcast.186), calls=%async_computation.15 | async-start | bytes 2097152
  329.7 8.1 %slice-start.9 = ((s8[5242880]{0:T(1024)(128)(4,1)}), s8[4194304]{0:T(1024)(128)(4,1)S(1)}, s32[]{:S(2)}) async-start(s8[5242880]{0:T(1024)(128)(4,1)} %bitcast.186), calls=%async_computation.16 | async-start | bytes 8388608
  377.8 18.1 %copy-start.1 = (s32[160]{0:T(256)S(1)}, s32[160]{0:T(256)}, u32[]{:S(2)}) copy-start(s32[160]{0:T(256)} %reshape.368) | copy-start | bytes 1924
  415.1 129.7 %all-to-all-start.3 = ((bf16[3,16,8192]{2,0,1:T(4,128)(2,1)}), bf16[3,16,8192]{2,0,1:T(4,128)(2,1)}, u32[]{:S(2)}, u32[]{:S(2)}) async-start(bf16[3,16,8192]{2,0,1:T(4,128)(2,1)} %copy.93), calls=%async_computation.3 | async-start | bytes 2097152 | tf_op jit(solution)/shard_map/all_to_all | solution.py:219
  430.6 14.6 %slice-start = ((s8[5242880]{0:T(1024)(128)(4,1)}), s8[1048576]{0:T(1024)(128)(4,1)S(1)}, s32[]{:S(2)}) async-start(s8[5242880]{0:T(1024)(128)(4,1)} %bitcast.166), calls=%async_computation.7 | async-start | bytes 2097152
  437.2 8.0 %slice-start.1 = ((s8[5242880]{0:T(1024)(128)(4,1)}), s8[4194304]{0:T(1024)(128)(4,1)S(1)}, s32[]{:S(2)}) async-start(s8[5242880]{0:T(1024)(128)(4,1)} %bitcast.166), calls=%async_computation.8 | async-start | bytes 8388608
  451.5 14.7 %slice-start.2 = ((s8[5242880]{0:T(1024)(128)(4,1)}), s8[1048576]{0:T(1024)(128)(4,1)S(1)}, s32[]{:S(2)}) async-start(s8[5242880]{0:T(1024)(128)(4,1)} %bitcast.168), calls=%async_computation.9 | async-start | bytes 2097152
  458.3 8.0 %slice-start.3 = ((s8[5242880]{0:T(1024)(128)(4,1)}), s8[4194304]{0:T(1024)(128)(4,1)S(1)}, s32[]{:S(2)}) async-start(s8[5242880]{0:T(1024)(128)(4,1)} %bitcast.168), calls=%async_computation.10 | async-start | bytes 8388608
  523.5 18.3 %copy-start.12 = (bf16[3,16,128,64]{2,3,1,0:T(8,128)(2,1)S(1)}, bf16[3,16,128,64]{2,3,1,0:T(8,128)(2,1)}, u32[]{:S(2)}) copy-start(bf16[3,16,128,64]{2,3,1,0:T(8,128)(2,1)} %convert.6) | copy-start | bytes 2359300
  541.9 9.2 %copy-start.28 = (s32[48]{0:T(128)S(1)}, s32[48]{0:T(128)}, u32[]{:S(2)}) copy-start(s32[48]{0:T(128)} %constant.261) | copy-start | bytes 580
  544.8 136.1 %all-to-all-start.4 = ((bf16[3,16,16384]{2,0,1:T(4,128)(2,1)}), bf16[3,16,16384]{2,0,1:T(4,128)(2,1)S(1)}, u32[]{:S(2)}, u32[]{:S(2)}) async-start(bf16[3,16,16384]{2,0,1:T(4,128)(2,1)} %reshape.439), calls=%async_computation.4 | async-start | bytes 4194304 | tf_op jit(solution)/shard_map/all_to_all | solution.py:220
  551.0 125.8 %all-reduce.11.cloned.1.call-start = ((), (), s32[]{:S(2)}) async-start(), calls=%async_computation.6 | async-start | bytes 3145728 | tf_op jit(solution)/shard_map/psum | solution.py:172
  552.9 7.9 %copy-start.19 = (bf16[128,64]{0,1:T(8,128)(2,1)S(1)}, bf16[128,64]{0,1:T(8,128)(2,1)}, u32[]{:S(2)}) copy-start(bf16[128,64]{0,1:T(8,128)(2,1)} %copy-done.18) | copy-start | bytes 49156
  554.8 8.4 %copy-start.8 = (bf16[128,3072]{1,0:T(8,128)(2,1)S(1)}, bf16[128,3072]{1,0:T(8,128)(2,1)}, u32[]{:S(2)}) copy-start(bf16[128,3072]{1,0:T(8,128)(2,1)} %param.19) | copy-start | bytes 2359300
Sparse Core Ops, SparseCore 0:
  565.8 110.8 all-reduce.10
where the time goes:
time: 718 us; the launch traced here: 707 us
  local copies, waits for them, and re-layouts  252 us (35%)
  other arithmetic  182 us (25%)
  waiting for transfers between devices  121 us (17%)
  matrix products  93.7 us (13%)
  starting transfers between devices  43.2 us (6%)
  between operations  15.2 us (2%)
    psum x1, waiting for transfers between devices, shards(): grad_down, grad_up = lax.psum((down_term, up_term), 'seq')  101 us
    scatter-add x3, other arithmetic, shards(): value_sums.at[slot_now, item_blocks]  54.6 us
    scatter-add x3, other arithmetic, shards(): key_sums.at[slot_now, item_blocks].add(key_grad.reshape(-1, KB, BLOCK, E))  54.4 us
    reshape x6, local copies, waits for them, and re-layouts, shards(): key_grad.reshape(-1, KB, BLOCK, E)  43.6 us
    reshape x6, local copies, waits for them, and re-layouts, shards(): value_grad.reshape(-1, KB, BLOCK, E)  43.6 us
    unnamed x94, local copies, waits for them, and re-layouts  31 us
    dot_general x3, matrix products, shards(): jnp.einsum('qrk,qke->qre', weights, gathered[..., E:], preferred_element_...  27.8 us
    dot_general x3, matrix products, shards(): jnp.einsum('qre,qke->qrk', grad_item, gathered[..., E:], preferred_elemen...  23.8 us
  transfers between devices with their start and end apart: 7, of which 4 were waited for; matrix products, arithmetic and copies ran while one was open for 53% of the time, Pallas kernels for 0%

commit v1 on v0

--- a/solution.py
+++ b/solution.py
@@ -2,6 +2,8 @@
 import jax.numpy as jnp
 import numpy as np
 from jax import lax
+from jax.experimental import pallas as pl
+from jax.experimental.pallas import tpu as pltpu
 from jax.sharding import PartitionSpec as P
 
 H = 48
@@ -70,7 +72,7 @@
     return buffer.reshape(slot_total, per_source * segments, -1)
 
 
-def shards(
+def segmented(
     qkv, output_gradient, adapter_down_weight, adapter_up_weight, listed_key_blocks, key_block_count
 ):
     device_total = lax.axis_size("seq")
@@ -237,6 +239,270 @@
     return (grad_qkv, grad_down * rescale, grad_up * rescale)
 
 
+LOG2E = 1.4426950408889634
+ROLL = E
+
+
+def low_lanes(rows):
+    return lax.broadcasted_iota(jnp.int32, (rows, 2 * E), 1) < E
+
+
+def swap(tile):
+    return pltpu.roll(tile, ROLL, 1)
+
+
+def pack_kernel(qkv_ref, grad_ref, up_ref, send_ref, pulled_ref):
+    low = low_lanes(BLOCK)
+    for pair in range(H // 2):
+        at = pair * 2 * E
+        query, key, value = (
+            qkv_ref[:, part * H * E + at : part * H * E + at + 2 * E].astype(jnp.float32)
+            for part in range(3)
+        )
+        grad = grad_ref[:, at : at + 2 * E].astype(jnp.float32)
+        for left, right, half in ((grad, query, 0), (value, key, 1)):
+            lanes = slice(half * 2 * E, half * 2 * E + 2 * E)
+            send_ref[2 * pair, :, lanes] = jnp.where(low, left, swap(right)).astype(jnp.bfloat16)
+            send_ref[2 * pair + 1, :, lanes] = jnp.where(low, swap(left), right).astype(
+                jnp.bfloat16
+            )
+    pulled_ref[...] = lax.dot_general(
+        grad_ref[...], up_ref[...], (((1,), (1,)), ((), ())), preferred_element_type=jnp.float32
+    ).astype(jnp.bfloat16)
+
+
+def head_kernel(
+    lists_ref, counts_ref, packed_ref, pulled_ref, wide_ref, down_ref,
+    out_ref, grad_down_ref,
+    sums, adapted, flipped, flipped_keyval, gathered, gathered_flip, attended, lowrank,
+):
+    head = pl.program_id(0)
+    block_total = packed_ref.shape[0]
+    low = low_lanes(BLOCK)
+    top = lax.broadcasted_iota(jnp.int32, (2 * E, BLOCK), 0) < E
+    live = counts_ref[head]
+
+    def prepare(block, carry):
+        rows = pl.ds(pl.multiple_of(block * BLOCK, BLOCK), BLOCK)
+        grad_query = packed_ref[block, 0, :, : 2 * E].astype(jnp.float32)
+        extra = jnp.dot(pulled_ref[rows, :], wide_ref[0], preferred_element_type=jnp.float32)
+        full = (grad_query + extra).astype(jnp.bfloat16)
+        adapted[block] = full
+        flipped[block] = full.astype(jnp.float32).T.astype(jnp.bfloat16)
+        flipped_keyval[block] = (
+            packed_ref[block, 0, :, 2 * E :].astype(jnp.float32).T.astype(jnp.bfloat16)
+        )
+        sums[head, block] = jnp.zeros((BLOCK, 2 * E), jnp.float32)
+        return carry
+
+    lax.fori_loop(0, block_total, prepare, 0)
+
+    def attend(block, carry):
+        cols = pl.ds(pl.multiple_of(block * BLOCK, BLOCK), BLOCK)
+        zero = jnp.zeros((BLOCK, 2 * E), jnp.bfloat16)
+        for slot in range(KB):
+            listed = lists_ref[head, block, slot]
+            gathered[slot * BLOCK : (slot + 1) * BLOCK, :] = packed_ref[listed, 0, :, 2 * E :]
+            gathered_flip[:, slot * BLOCK : (slot + 1) * BLOCK] = flipped_keyval[listed]
+        turned = flipped[block]
+        pair = jnp.concatenate([jnp.where(top, turned, zero), jnp.where(top, zero, turned)], axis=1)
+        both = jnp.dot(gathered[...], pair, preferred_element_type=jnp.float32)
+        dotted = both[:, :BLOCK]
+        slots = lax.broadcasted_iota(jnp.int32, (KB * BLOCK, BLOCK), 0)
+        scores = jnp.where(slots < live * BLOCK, both[:, BLOCK:], -jnp.inf)
+        peak = jnp.max(scores, axis=0, keepdims=True)
+        raised = jnp.exp2((scores - peak) * (LOG2E * E**-0.5))
+        weights = (raised * (1.0 / jnp.sum(raised, axis=0, keepdims=True))).astype(jnp.bfloat16)
+        output = jnp.dot(
+            gathered_flip[:E, :], weights, preferred_element_type=jnp.float32
+        ).astype(jnp.bfloat16)
+        attended[:, cols] = output
+        delta = jnp.sum(
+            output.astype(jnp.float32) * turned[:E].astype(jnp.float32), axis=0, keepdims=True
+        )
+        score_grad = (weights.astype(jnp.float32) * (dotted - delta)).astype(jnp.bfloat16)
+        query_grad = (
+            jnp.dot(gathered_flip[E:, :], score_grad, preferred_element_type=jnp.float32)
+            * E**-0.5
+        )
+        query_wide = jnp.concatenate([query_grad, jnp.zeros_like(query_grad)], axis=0).T
+        out_ref[block, head] = query_wide.astype(jnp.bfloat16)
+        mixed = adapted[block]
+        stacked = jnp.concatenate([jnp.where(low, mixed, zero), jnp.where(low, zero, mixed)], axis=0)
+        partial = jnp.dot(
+            jnp.concatenate([weights, score_grad], axis=1),
+            stacked,
+            preferred_element_type=jnp.float32,
+        )
+        for slot in range(KB):
+            listed = lists_ref[head, block, slot]
+            sums[head, listed] += partial[slot * BLOCK : (slot + 1) * BLOCK]
+        return carry
+
+    lax.fori_loop(0, block_total, attend, 0)
+
+    def finish(block, carry):
+        key_value = sums[head, block]
+        out_ref[block, head] = jnp.where(
+            low, out_ref[block, head].astype(jnp.float32), key_value * E**-0.5
+        ).astype(jnp.bfloat16)
+        return carry
+
+    lax.fori_loop(0, block_total, finish, 0)
+    grad_down_ref[0] = jnp.dot(
+        attended[...], pulled_ref[...], preferred_element_type=jnp.float32
+    ) * (block_total * BLOCK) ** (-0.5)
+    term = lax.dot_general(
+        down_ref[0], attended[...], (((0,), (0,)), ((), ())), preferred_element_type=jnp.float32
+    )
+
+    @pl.when(head == 0)
+    def _():
+        lowrank[...] = term
+
+    @pl.when(head > 0)
+    def _():
+        lowrank[...] += term
+
+    @pl.when(head == ITEMS_DEV - 1)
+    def _():
+        def tail(block, carry):
+            cols = pl.ds(pl.multiple_of(block * BLOCK, BLOCK), BLOCK)
+            out_ref[block, 3] = jnp.where(low, sums[0, block], swap(sums[1, block])).astype(
+                jnp.bfloat16
+            )
+            rank = lowrank[:, cols]
+            rank = jnp.concatenate([jnp.zeros_like(rank), rank], axis=0).T
+            out_ref[block, 4] = jnp.where(low, sums[2, block], rank).astype(jnp.bfloat16)
+            return carry
+
+        lax.fori_loop(0, block_total, tail, 0)
+
+
+def unpack_kernel(back_ref, out_ref, lowrank_ref):
+    low = low_lanes(BLOCK)
+    total = jnp.zeros((BLOCK, 2 * E), jnp.float32)
+
+    def tile(device, which):
+        return back_ref[device, which].astype(jnp.float32)
+
+    for pair in range(H // 2):
+        at = pair * 2 * E
+        first, second = 2 * pair, 2 * pair + 1
+        left = tile(first // ITEMS_DEV, first % ITEMS_DEV)
+        right = tile(second // ITEMS_DEV, second % ITEMS_DEV)
+        out_ref[:, at : at + 2 * E] = jnp.where(low, left, swap(right)).astype(jnp.bfloat16)
+        out_ref[:, H * E + at : H * E + at + 2 * E] = jnp.where(low, swap(left), right).astype(
+            jnp.bfloat16
+        )
+        placed = []
+        for head, want in ((first, 0), (second, 1)):
+            device, within = head // ITEMS_DEV, head % ITEMS_DEV
+            value = tile(device, 3 + within // 2)
+            placed.append(value if within % 2 == want else swap(value))
+        out_ref[:, 2 * H * E + at : 2 * H * E + at + 2 * E] = jnp.where(
+            low, placed[0], placed[1]
+        ).astype(jnp.bfloat16)
+    for device in range(back_ref.shape[0]):
+        total += tile(device, 4)
+    lowrank_ref[...] = total[:, E:].astype(jnp.bfloat16)
+
+
+def whole_heads(
+    qkv, output_gradient, adapter_down_weight, adapter_up_weight, listed_key_blocks, key_block_count
+):
+    device_total = lax.axis_size("seq")
+    me = lax.axis_index("seq")
+    vmem = pl.BlockSpec(memory_space=pltpu.VMEM)
+    params = pltpu.CompilerParams(vmem_limit_bytes=48 * 1024 * 1024)
+    send, pulled = pl.pallas_call(
+        pack_kernel,
+        out_shape=(
+            jax.ShapeDtypeStruct((H, BLOCK, 4 * E), jnp.bfloat16),
+            jax.ShapeDtypeStruct((BLOCK, adapter_up_weight.shape[0]), jnp.bfloat16),
+        ),
+        in_specs=[vmem] * 3,
+        out_specs=(vmem, vmem),
+        compiler_params=params,
+    )(qkv, output_gradient, adapter_up_weight)
+    pulled_all = lax.all_gather(pulled, "seq", axis=0, tiled=True)
+    packed = lax.all_to_all(
+        send.reshape(device_total, ITEMS_DEV, BLOCK, 4 * E), "seq", 0, 0, tiled=True
+    )
+    first = me * ITEMS_DEV
+    lists = lax.dynamic_slice_in_dim(listed_key_blocks, first, ITEMS_DEV, 0)
+    counts = lax.dynamic_slice_in_dim(key_block_count, first, ITEMS_DEV, 0)
+    down = lax.dynamic_slice_in_dim(adapter_down_weight, first * E, ITEMS_DEV * E, 0).reshape(
+        ITEMS_DEV, E, -1
+    )
+    rank = down.shape[-1]
+    wide = jnp.pad(jnp.swapaxes(down, 1, 2), ((0, 0), (0, 0), (0, E)))
+    tokens = device_total * BLOCK
+    back, grad_down = pl.pallas_call(
+        head_kernel,
+        grid_spec=pltpu.PrefetchScalarGridSpec(
+            num_scalar_prefetch=2,
+            grid=(ITEMS_DEV,),
+            in_specs=[
+                pl.BlockSpec((device_total, 1, BLOCK, 4 * E), lambda h, *_: (0, h, 0, 0)),
+                pl.BlockSpec((tokens, rank), lambda h, *_: (0, 0)),
+                pl.BlockSpec((1, rank, 2 * E), lambda h, *_: (h, 0, 0)),
+                pl.BlockSpec((1, E, rank), lambda h, *_: (h, 0, 0)),
+            ],
+            out_specs=[
+                pl.BlockSpec((device_total, 5, BLOCK, 2 * E), lambda h, *_: (0, 0, 0, 0)),
+                pl.BlockSpec((1, E, rank), lambda h, *_: (h, 0, 0)),
+            ],
+            scratch_shapes=[
+                pltpu.VMEM((ITEMS_DEV, device_total, BLOCK, 2 * E), jnp.float32),
+                pltpu.VMEM((device_total, BLOCK, 2 * E), jnp.bfloat16),
+                pltpu.VMEM((device_total, 2 * E, BLOCK), jnp.bfloat16),
+                pltpu.VMEM((device_total, 2 * E, BLOCK), jnp.bfloat16),
+                pltpu.VMEM((KB * BLOCK, 2 * E), jnp.bfloat16),
+                pltpu.VMEM((2 * E, KB * BLOCK), jnp.bfloat16),
+                pltpu.VMEM((E, tokens), jnp.bfloat16),
+                pltpu.VMEM((rank, tokens), jnp.float32),
+            ],
+        ),
+        out_shape=[
+            jax.ShapeDtypeStruct((device_total, 5, BLOCK, 2 * E), jnp.bfloat16),
+            jax.ShapeDtypeStruct((ITEMS_DEV, E, rank), jnp.float32),
+        ],
+        compiler_params=params,
+    )(lists, counts, packed, pulled_all, wide, down)
+    grad_down_all = lax.all_gather(
+        grad_down.reshape(ITEMS_DEV * E, rank), "seq", axis=0, tiled=True
+    )
+    returned = lax.all_to_all(back, "seq", 0, 0, tiled=True)
+    grad_qkv, lowrank = pl.pallas_call(
+        unpack_kernel,
+        out_shape=(
+            jax.ShapeDtypeStruct(qkv.shape, jnp.bfloat16),
+            jax.ShapeDtypeStruct((BLOCK, rank), jnp.bfloat16),
+        ),
+        in_specs=[vmem],
+        out_specs=(vmem, vmem),
+        compiler_params=params,
+    )(returned)
+    lowrank_all = lax.all_gather(lowrank, "seq", axis=0, tiled=True)
+    grad_up = jnp.einsum(
+        "str,shte->her",
+        lowrank_all.reshape(device_total, BLOCK, rank),
+        packed[..., :E].astype(jnp.bfloat16),
+        preferred_element_type=jnp.float32,
+    ) * tokens ** (-0.5)
+    grad_up_all = lax.all_gather(
+        grad_up.reshape(ITEMS_DEV * E, rank), "seq", axis=0, tiled=True
+    )
+    return (grad_qkv, grad_down_all, grad_up_all.T)
+
+
+def shards(qkv, *others):
+    if ITEMS_DEV * lax.axis_size("seq") == H and qkv.shape[0] == BLOCK:
+        return whole_heads(qkv, *others)
+    return segmented(qkv, *others)
+
+
 def solution(mesh):
     return jax.shard_map(
         shards,

time: 718 us -> 316 us (0.44); the launches traced: 707 us -> 316 us
  local copies, waits for them, and re-layouts: 252 us -> 12.2 us
  blocking collectives: 0 us -> 193 us
  other arithmetic: 182 us -> 0 us
  waiting for transfers between devices: 121 us -> 0.01 us
  Pallas kernels: 0 us -> 93.4 us
  matrix products: 93.7 us -> 1.99 us
  starting transfers between devices: 43.2 us -> 14.5 us
  between operations: 15.2 us -> 0.76 us
    all_gather x0 -> x4, blocking collectives: none -> 193 us  [the longest x1 78.4 us: whole_heads(): pulled_all = lax.all_gather(pulled, 'seq', axis=0, tiled=True)]
    scatter-add x6 -> x0, other arithmetic: 109 us -> none  [the longest x3 54.6 us: shards(): value_sums.at[slot_now, item_blocks]]
    psum x1 -> x0, waiting for transfers between devices: 101 us -> none  [shards(): grad_down, grad_up = lax.psum((down_term, up_term), 'seq')]
    reshape x22 -> x0, local copies, waits for them, and re-layouts: 100 us -> none  [the longest x6 43.6 us: shards(): key_grad.reshape(-1, KB, BLOCK, E)]
    pallas_call x0 -> x3, Pallas kernels: none -> 93.4 us  [the longest x1 88 us: whole_heads(): pl.pallas_call(head_kernel, grid_spec=pltpu.PrefetchScalarGridSpec(num_sc...]
    dot_general x22 -> x1, matrix products: 93.7 us -> 1.99 us  [whole_heads(): jnp.einsum('str,shte->her', lowrank_all.reshape(device_total, BLOCK, rank...]
    gather x16 -> x0, local copies, waits for them, and re-layouts: 39.8 us -> none  [the longest x3 23.5 us: shards(): jnp.take(keyval_item, item_blocks, axis=0).reshape(-1, KB * BLOCK, 2 * E)]
    all_to_all x6 -> x2, starting transfers between devices: 43.1 us -> 14.5 us  [the longest x1 7.56 us: whole_heads(): lax.all_to_all(send.reshape(device_total, ITEMS_DEV, BLOCK, 4 * E), 'seq'...]
  transfers between devices with their start and end apart: 7 -> 2, of which waited for: 4 -> 0; matrix products, arithmetic and copies ran while one was open for 53% -> 2% of each run, Pallas kernels for 0% -> 0%
where the time goes in v1:
time: 316 us
  blocking collectives  193 us (61%)
  Pallas kernels  93.4 us (30%)
  starting transfers between devices  14.5 us (5%)
  local copies, waits for them, and re-layouts  12.2 us (4%)
    pallas_call x1, Pallas kernels, whole_heads(): pl.pallas_call(head_kernel, grid_spec=pltpu.PrefetchScalarGridSpec(num_sc...  88 us
    all_gather x1, blocking collectives, whole_heads(): pulled_all = lax.all_gather(pulled, 'seq', axis=0, tiled=True)  78.4 us
    all_gather x1, blocking collectives, whole_heads(): lax.all_gather(grad_down.reshape(ITEMS_DEV * E, rank), 'seq', axis=0, til...  70.4 us
    all_gather x1, blocking collectives, whole_heads(): lowrank_all = lax.all_gather(lowrank, 'seq', axis=0, tiled=True)  23.2 us
    all_gather x1, blocking collectives, whole_heads(): lax.all_gather(grad_up.reshape(ITEMS_DEV * E, rank), 'seq', axis=0, tiled...  20.7 us
    unnamed x20, local copies, waits for them, and re-layouts  9.6 us
    all_to_all x1, starting transfers between devices, whole_heads(): lax.all_to_all(send.reshape(device_total, ITEMS_DEV, BLOCK, 4 * E), 'seq'...  7.56 us
    all_to_all x1, starting transfers between devices, whole_heads(): returned = lax.all_to_all(back, 'seq', 0, 0, tiled=True)  6.98 us
  transfers between devices with their start and end apart: 2, of which 0 were waited for; matrix products, arithmetic and copies ran while one was open for 2% of the time, Pallas kernels for 0%

profile of v1, /device:TPU:0, one launch (start us, length us, event | category | flops | bytes accessed | tf_op | source)
XLA Modules:
  0.0 315.5 jit_solution(17572314688778659959)
XLA Ops:
  0.6 0.0 copy-start
  0.6 0.0 copy-start.2
  0.7 1.7 copy-done.2
  2.4 0.0 copy-start.3
  2.4 1.1 copy-done.3
  3.5 0.0 copy-start.4
  3.5 1.0 copy-done.4
  4.5 3.0 shard_map.85
  7.5 0.0 copy-start.6
  7.5 0.0 copy-start.5
  7.5 7.6 %all-to-all-start = ((bf16[16,3,128,256]{3,2,1,0:T(8,128)(2,1)}), bf16[16,3,128,256]{3,2,1,0:T(8,128)(2,1)}, u32[]{:S(2)}, u32[]{:S(2)}) async-start(bf16[16,3,128,256]{3,2,1,0:T(8,128)(2,1)} %bitcast.24), calls=%async_computation | async-start | bytes 6291456 | tf_op jit(solution)/shard_map/all_to_all | solution.py:429
  15.1 0.0 copy-done
  15.1 0.1 constant_dynamic-slice_fusion
  15.2 0.1 copy.24
  15.3 0.1 copy.37
  15.4 0.0 copy-done.6
  15.4 0.1 dynamic_slice.10.counts_ref
  15.5 0.0 copy-done.5
  15.5 0.1 constant_dynamic-slice_fusion.1
  15.6 0.2 copy.36.lists_ref
  15.8 78.4 %all_gather.12.pulled_ref = bf16[2048,64]{1,0:T(8,128)(2,1)S(1)} all-gather(bf16[128,64]{1,0:T(8,128)(2,1)S(1)} %get-tuple-element.10), channel_id=1, replica_groups=mesh['groups'=2,'seq'=16] {'seq'}, dimensions={0}, use_global_device_ids=true | all-gather | bytes 278528 | tf_op jit(solution)/shard_map/all_gather | solution.py:428
  94.2 0.0 all-to-all-done.packed_ref
  94.2 88.0 %shard_map.86 = (bf16[16,5,128,128]{3,2,1,0:T(8,128)(2,1)S(1)}, f32[3,64,64]{2,1,0:T(8,128)S(1)}) custom-call(s32[3,16,10]{2,1,0:T(8,128)S(1)} %copy.36.lists_ref, s32[3]{0:T(128)S(1)} %dynamic_slice.10.counts_ref, bf16[16,3,128,256]{3,2,1,0:T(8,128)(2,1)} %all-to-all-done.packed_ref, bf16[2048,64]{1,0:T(8,128)(2,1)S(1)} %all_gather.12.pulled_ref, ...), custom_call_target="tpu_custom_call" | custom-call | tf_op jit(solution)/shard_map/pallas_call | solution.py:441
  182.2 0.0 copy-start.1
  182.2 1.5 copy-done.1
  183.7 7.0 %all-to-all-start.1 = ((bf16[16,5,128,128]{3,2,1,0:T(8,128)(2,1)}), bf16[16,5,128,128]{3,2,1,0:T(8,128)(2,1)S(1)}, u32[]{:S(2)}, u32[]{:S(2)}) async-start(bf16[16,5,128,128]{3,2,1,0:T(8,128)(2,1)} %copy-done.1), calls=%async_computation.1 | async-start | bytes 5242880 | tf_op jit(solution)/shard_map/all_to_all | solution.py:476
  190.7 0.1 copy.26
  190.8 70.4 %all-gather = f32[16,192,64]{1,2,0:T(8,128)S(1)} all-gather(f32[1,192,64]{1,2,0:T(8,128)S(1)} %copy.26), channel_id=1, replica_groups=mesh['groups'=2,'seq'=16] {'seq'}, dimensions={0}, use_global_device_ids=true | all-gather | bytes 835584 | tf_op jit(solution)/shard_map/all_gather | solution.py:473
  261.2 1.6 copy.27
  262.8 2.5 reshape.27
  265.3 0.0 all-to-all-done.1.back_ref
  265.3 2.4 shard_map.87
  267.7 23.2 %all_gather.14 = bf16[2048,64]{1,0:T(8,128)(2,1)S(1)} all-gather(bf16[128,64]{1,0:T(8,128)(2,1)S(1)} %get-tuple-element.14), channel_id=1, replica_groups=mesh['groups'=2,'seq'=16] {'seq'}, dimensions={0}, use_global_device_ids=true | all-gather | bytes 278528 | tf_op jit(solution)/shard_map/all_gather | solution.py:487
  290.9 2.0 fusion.5
  292.9 0.1 copy.30
  293.0 20.7 %all-gather.1 = f32[16,192,64]{1,2,0:T(8,128)S(1)} all-gather(f32[1,192,64]{1,2,0:T(8,128)S(1)} %copy.30), channel_id=1, replica_groups=mesh['groups'=2,'seq'=16] {'seq'}, dimensions={0}, use_global_device_ids=true | all-gather | bytes 835584 | tf_op jit(solution)/shard_map/all_gather | solution.py:494
  313.7 0.6 copy.31
  314.3 1.3 reshape.29
  (1 shorter events, 0.0 us)
Async XLA Ops:
  0.6 14.5 %copy-start = (bf16[3072,64]{0,1:T(8,128)(2,1)S(1)}, bf16[3072,64]{0,1:T(8,128)(2,1)}, u32[]{:S(2)}) copy-start(bf16[3072,64]{0,1:T(8,128)(2,1)} %param.8) | copy-start | bytes 1179652
  0.6 1.7 copy-start.2
  2.4 1.1 copy-start.3
  3.5 1.0 copy-start.4
  7.5 7.9 %copy-start.6 = (s32[48]{0:T(128)S(1)}, s32[48]{0:T(128)}, u32[]{:S(2)}) copy-start(s32[48]{0:T(128)} %param.11) | copy-start | bytes 580
  7.5 8.0 %copy-start.5 = (s32[48,16,10]{0,1,2:T(8,128)S(1)}, s32[48,16,10]{0,1,2:T(8,128)}, u32[]{:S(2)}) copy-start(s32[48,16,10]{0,1,2:T(8,128)} %param.10) | copy-start | bytes 92164
  7.5 86.7 %all-to-all-start = ((bf16[16,3,128,256]{3,2,1,0:T(8,128)(2,1)}), bf16[16,3,128,256]{3,2,1,0:T(8,128)(2,1)}, u32[]{:S(2)}, u32[]{:S(2)}) async-start(bf16[16,3,128,256]{3,2,1,0:T(8,128)(2,1)} %bitcast.24), calls=%async_computation | async-start | bytes 6291456 | tf_op jit(solution)/shard_map/all_to_all | solution.py:429
  182.2 1.5 copy-start.1
  183.7 81.6 %all-to-all-start.1 = ((bf16[16,5,128,128]{3,2,1,0:T(8,128)(2,1)}), bf16[16,5,128,128]{3,2,1,0:T(8,128)(2,1)S(1)}, u32[]{:S(2)}, u32[]{:S(2)}) async-start(bf16[16,5,128,128]{3,2,1,0:T(8,128)(2,1)} %copy-done.1), calls=%async_computation.1 | async-start | bytes 5242880 | tf_op jit(solution)/shard_map/all_to_all | solution.py:476

commit v2 on v0

--- a/solution.py
+++ b/solution.py
@@ -1,7 +1,11 @@
+import functools
+
 import jax
 import jax.numpy as jnp
 import numpy as np
 from jax import lax
+from jax.experimental import pallas as pl
+from jax.experimental.pallas import tpu as pltpu
 from jax.sharding import PartitionSpec as P
 
 H = 48
@@ -70,7 +74,7 @@
     return buffer.reshape(slot_total, per_source * segments, -1)
 
 
-def shards(
+def segmented(
     qkv, output_gradient, adapter_down_weight, adapter_up_weight, listed_key_blocks, key_block_count
 ):
     device_total = lax.axis_size("seq")
@@ -237,6 +241,350 @@
     return (grad_qkv, grad_down * rescale, grad_up * rescale)
 
 
+LOG2E = 1.4426950408889634
+ROLL = E
+
+
+def low_lanes(rows):
+    return lax.broadcasted_iota(jnp.int32, (rows, 2 * E), 1) < E
+
+
+def swap(tile):
+    return pltpu.roll(tile, ROLL, 1)
+
+
+def pack_kernel(qkv_ref, grad_ref, up_ref, *send_refs):
+    low = low_lanes(BLOCK)
+    for pair in range(H // 2):
+        at = pair * 2 * E
+        query, key, value = (
+            qkv_ref[:, part * H * E + at : part * H * E + at + 2 * E].astype(jnp.float32)
+            for part in range(3)
+        )
+        grad = grad_ref[:, at : at + 2 * E].astype(jnp.float32)
+        for left, right, half in ((grad, query, 0), (value, key, 1)):
+            lanes = slice(half * 2 * E, half * 2 * E + 2 * E)
+            for head, tile in (
+                (2 * pair, jnp.where(low, left, swap(right))),
+                (2 * pair + 1, jnp.where(low, swap(left), right)),
+            ):
+                send_refs[head % ITEMS_DEV][head // ITEMS_DEV, :BLOCK, lanes] = tile.astype(
+                    jnp.bfloat16
+                )
+    pulled = lax.dot_general(
+        grad_ref[...], up_ref[...], (((1,), (1,)), ((), ())), preferred_element_type=jnp.float32
+    )
+    folded = jnp.concatenate(
+        [pulled[part * BLOCK // 4 : (part + 1) * BLOCK // 4] for part in range(4)], axis=1
+    ).astype(jnp.bfloat16)
+    for device in range(send_refs[0].shape[0]):
+        send_refs[0][device, BLOCK:, :] = folded
+
+
+def head_kernel(forward, backward, unfold, *refs):
+    refs = list(refs)
+    lists_ref, counts_ref, packed_ref, wide_ref, down_ref = refs[:5]
+    del refs[:5]
+    block_total = packed_ref.shape[0]
+    pulled_in = None if unfold else refs.pop(0)
+    lowrank_in = refs.pop(0) if forward and not unfold else None
+    if backward:
+        rows_ref, sums = refs.pop(0), refs.pop(0)
+    if unfold:
+        pulled_ref = refs.pop(0)
+    else:
+        pulled_ref = pulled_in
+    if forward:
+        grad_down_ref, lowrank_ref = refs.pop(0), refs.pop(0)
+    adapted, flipped, flipped_keyval, gathered, gathered_flip, attended = refs
+    low = low_lanes(BLOCK)
+    top = lax.broadcasted_iota(jnp.int32, (2 * E, BLOCK), 0) < E
+    live = counts_ref[0]
+    zero = jnp.zeros((BLOCK, 2 * E), jnp.bfloat16)
+
+    def prepare(block, carry):
+        rows = pl.ds(pl.multiple_of(block * BLOCK, BLOCK), BLOCK)
+        if unfold:
+            folded = packed_ref[block, BLOCK:, :]
+            pulled_ref[rows, :] = jnp.concatenate(
+                [folded[:, part * E : (part + 1) * E] for part in range(4)], axis=0
+            )
+        grad_query = packed_ref[block, :BLOCK, : 2 * E].astype(jnp.float32)
+        extra = jnp.dot(pulled_ref[rows, :], wide_ref[...], preferred_element_type=jnp.float32)
+        full = (grad_query + extra).astype(jnp.bfloat16)
+        adapted[block] = full
+        flipped[block] = full.astype(jnp.float32).T.astype(jnp.bfloat16)
+        flipped_keyval[block] = (
+            packed_ref[block, :BLOCK, 2 * E :].astype(jnp.float32).T.astype(jnp.bfloat16)
+        )
+        if backward:
+            sums[block] = jnp.zeros((BLOCK, 2 * E), jnp.float32)
+        return carry
+
+    lax.fori_loop(0, block_total, prepare, 0)
+
+    def attend(step, carry):
+        blocks = [2 * step, 2 * step + 1]
+        for side, block in enumerate(blocks):
+            for slot in range(KB):
+                listed = lists_ref[block, slot]
+                span = slice(slot * BLOCK, (slot + 1) * BLOCK)
+                gathered[side, span, :] = packed_ref[listed, :BLOCK, 2 * E :]
+                gathered_flip[side, :, span] = flipped_keyval[listed]
+        turned = [flipped[block] for block in blocks]
+        both = []
+        for side in range(2):
+            pair = jnp.concatenate(
+                [jnp.where(top, turned[side], zero), jnp.where(top, zero, turned[side])], axis=1
+            )
+            both.append(jnp.dot(gathered[side], pair, preferred_element_type=jnp.float32))
+        slots = lax.broadcasted_iota(jnp.int32, (KB * BLOCK, BLOCK), 0)
+        weights = []
+        for side in range(2):
+            scores = jnp.where(slots < live * BLOCK, both[side][:, BLOCK:], -jnp.inf)
+            peak = jnp.max(scores, axis=0, keepdims=True)
+            raised = jnp.exp2((scores - peak) * (LOG2E * E**-0.5))
+            weights.append(
+                (raised * (1.0 / jnp.sum(raised, axis=0, keepdims=True))).astype(jnp.bfloat16)
+            )
+        outputs = [
+            jnp.dot(
+                gathered_flip[side, :E, :], weights[side], preferred_element_type=jnp.float32
+            ).astype(jnp.bfloat16)
+            for side in range(2)
+        ]
+        if forward:
+            cols = pl.ds(pl.multiple_of(step * 2 * BLOCK, 2 * BLOCK), 2 * BLOCK)
+            attended[:, cols] = jnp.concatenate(outputs, axis=1)
+        if not backward:
+            return carry
+        score_grads = []
+        for side in range(2):
+            delta = jnp.sum(
+                outputs[side].astype(jnp.float32) * turned[side][:E].astype(jnp.float32),
+                axis=0,
+                keepdims=True,
+            )
+            score_grads.append(
+                (weights[side].astype(jnp.float32) * (both[side][:, :BLOCK] - delta)).astype(
+                    jnp.bfloat16
+                )
+            )
+        partials = []
+        for side, block in enumerate(blocks):
+            query_grad = (
+                jnp.dot(
+                    gathered_flip[side, E:, :],
+                    score_grads[side],
+                    preferred_element_type=jnp.float32,
+                )
+                * E**-0.5
+            )
+            rows_ref[block] = jnp.concatenate(
+                [query_grad, jnp.zeros_like(query_grad)], axis=0
+            ).T.astype(jnp.bfloat16)
+            mixed = adapted[block]
+            stacked = jnp.concatenate(
+                [jnp.where(low, mixed, zero), jnp.where(low, zero, mixed)], axis=0
+            )
+            partials.append(
+                jnp.dot(
+                    jnp.concatenate([weights[side], score_grads[side]], axis=1),
+                    stacked,
+                    preferred_element_type=jnp.float32,
+                )
+            )
+        for side, block in enumerate(blocks):
+            for slot in range(KB):
+                listed = lists_ref[block, slot]
+                sums[listed] += partials[side][slot * BLOCK : (slot + 1) * BLOCK]
+        return carry
+
+    lax.fori_loop(0, block_total // 2, attend, 0)
+
+    if backward:
+        def finish(block, carry):
+            rows_ref[block] = jnp.where(
+                low, rows_ref[block].astype(jnp.float32), sums[block] * E**-0.5
+            ).astype(jnp.bfloat16)
+            return carry
+
+        lax.fori_loop(0, block_total, finish, 0)
+    if forward:
+        grad_down_ref[...] = jnp.dot(
+            attended[...], pulled_ref[...], preferred_element_type=jnp.float32
+        ) * (block_total * BLOCK) ** (-0.5)
+        term = lax.dot_general(
+            down_ref[...], attended[...], (((0,), (0,)), ((), ())),
+            preferred_element_type=jnp.float32,
+        )
+        lowrank_ref[...] = term if unfold else term + lowrank_in[...]
+
+
+def head_pass(forward, backward, unfold, lists, counts, packed, wide, down, *extra):
+    blocks = packed.shape[0]
+    rank = down.shape[-1]
+    tokens = blocks * BLOCK
+    vmem = pl.BlockSpec(memory_space=pltpu.VMEM)
+    smem = pl.BlockSpec(memory_space=pltpu.SMEM)
+    outs = []
+    if backward:
+        outs.append(jax.ShapeDtypeStruct((blocks, BLOCK, 2 * E), jnp.bfloat16))
+        outs.append(jax.ShapeDtypeStruct((blocks, BLOCK, 2 * E), jnp.float32))
+    if unfold:
+        outs.append(jax.ShapeDtypeStruct((tokens, rank), jnp.bfloat16))
+    if forward:
+        outs.append(jax.ShapeDtypeStruct((E, rank), jnp.float32))
+        outs.append(jax.ShapeDtypeStruct((rank, tokens), jnp.float32))
+    return pl.pallas_call(
+        functools.partial(head_kernel, forward, backward, unfold),
+        out_shape=outs,
+        in_specs=[smem, smem] + [vmem] * (3 + len(extra)),
+        out_specs=[vmem] * len(outs),
+        scratch_shapes=[
+            pltpu.VMEM((blocks, BLOCK, 2 * E), jnp.bfloat16),
+            pltpu.VMEM((blocks, 2 * E, BLOCK), jnp.bfloat16),
+            pltpu.VMEM((blocks, 2 * E, BLOCK), jnp.bfloat16),
+            pltpu.VMEM((2, KB * BLOCK, 2 * E), jnp.bfloat16),
+            pltpu.VMEM((2, 2 * E, KB * BLOCK), jnp.bfloat16),
+            pltpu.VMEM((E, tokens), jnp.bfloat16),
+        ],
+        compiler_params=pltpu.CompilerParams(vmem_limit_bytes=40 * 1024 * 1024),
+        cost_estimate=pl.CostEstimate(
+            flops=(20 if backward else 8) * 10**9, bytes_accessed=4 * 10**6, transcendentals=0
+        ),
+    )(lists, counts, packed, wide, down, *extra)
+
+
+def rank_kernel(lowrank_ref, first_ref, second_ref, third_ref, out_ref):
+    for within, packed_ref in enumerate((first_ref, second_ref, third_ref)):
+        total = jnp.zeros((out_ref.shape[1], 2 * E), jnp.float32)
+        for block in range(packed_ref.shape[0]):
+            total += jnp.dot(
+                lowrank_ref[block],
+                packed_ref[block, :BLOCK, : 2 * E],
+                preferred_element_type=jnp.float32,
+            )
+        out_ref[within] = total * (packed_ref.shape[0] * BLOCK) ** (-0.5)
+
+
+def unpack_kernel(early_ref, late_ref, out_ref):
+    def tile(device, which):
+        if which < 3:
+            return early_ref[device, which].astype(jnp.float32)
+        return late_ref[device, which - 3].astype(jnp.float32)
+
+    low = low_lanes(BLOCK)
+    for pair in range(H // 2):
+        at = pair * 2 * E
+        left, right = (
+            tile(head // ITEMS_DEV, (0, 1, 3)[head % ITEMS_DEV])
+            for head in (2 * pair, 2 * pair + 1)
+        )
+        out_ref[:, at : at + 2 * E] = jnp.where(low, left, swap(right)).astype(jnp.bfloat16)
+        out_ref[:, H * E + at : H * E + at + 2 * E] = jnp.where(low, swap(left), right).astype(
+            jnp.bfloat16
+        )
+        placed = []
+        for want in range(2):
+            head = 2 * pair + want
+            device, within = head // ITEMS_DEV, head % ITEMS_DEV
+            value = tile(device, 2 if within < 2 else 4)
+            placed.append(value if within % 2 == want else swap(value))
+        out_ref[:, 2 * H * E + at : 2 * H * E + at + 2 * E] = jnp.where(
+            low, placed[0], placed[1]
+        ).astype(jnp.bfloat16)
+
+
+def whole_heads(
+    qkv, output_gradient, adapter_down_weight, adapter_up_weight, listed_key_blocks, key_block_count
+):
+    device_total = lax.axis_size("seq")
+    me = lax.axis_index("seq")
+    rank = adapter_up_weight.shape[0]
+    vmem = pl.BlockSpec(memory_space=pltpu.VMEM)
+    params = pltpu.CompilerParams(vmem_limit_bytes=40 * 1024 * 1024)
+
+    def exchange(array):
+        return lax.all_to_all(array, "seq", 0, 0, tiled=True)
+
+    sends = pl.pallas_call(
+        pack_kernel,
+        out_shape=[
+            jax.ShapeDtypeStruct(
+                (device_total, BLOCK + (BLOCK // 4 if within == 0 else 0), 4 * E), jnp.bfloat16
+            )
+            for within in range(ITEMS_DEV)
+        ],
+        in_specs=[vmem] * 3,
+        out_specs=[vmem] * ITEMS_DEV,
+        compiler_params=params,
+    )(qkv, output_gradient, adapter_up_weight)
+    packed0 = exchange(sends[0])
+    first = me * ITEMS_DEV
+    lists = lax.dynamic_slice_in_dim(listed_key_blocks, first, ITEMS_DEV, 0)
+    counts = lax.dynamic_slice_in_dim(key_block_count, first, ITEMS_DEV, 0)
+    down = lax.dynamic_slice_in_dim(adapter_down_weight, first * E, ITEMS_DEV * E, 0).reshape(
+        ITEMS_DEV, E, rank
+    )
+    wide = jnp.pad(jnp.swapaxes(down, 1, 2), ((0, 0), (0, 0), (0, E)))
+    def own(within, packed):
+        return (
+            lists[within], counts[within : within + 1], packed, wide[within], down[within]
+        )
+
+    packed0, send1 = lax.optimization_barrier((packed0, sends[1]))
+    packed1 = exchange(send1)
+    rows0, sums0, pulled, down0, lowrank = head_pass(True, True, True, *own(0, packed0))
+    packed1, rows0, pulled, lowrank, send2 = lax.optimization_barrier(
+        (packed1, rows0, pulled, lowrank, sends[2])
+    )
+    packed2 = exchange(send2)
+    rows1, sums1, down1, lowrank = head_pass(
+        True, True, False, *own(1, packed1), pulled, lowrank
+    )
+    values = jnp.concatenate([sums0[..., :E], sums1[..., :E]], axis=-1).astype(jnp.bfloat16)
+    early = jnp.stack([rows0, rows1, values], axis=1)
+    early, packed2 = lax.optimization_barrier((early, packed2))
+    back1 = exchange(early)
+    down2, lowrank = head_pass(True, False, False, *own(2, packed2), pulled, lowrank)
+    rows2, sums2 = head_pass(False, True, False, *own(2, packed2), pulled)
+    spread = jnp.swapaxes(
+        lowrank.astype(jnp.bfloat16).reshape(rank, device_total, BLOCK), 0, 1
+    )
+    late = jnp.stack([rows2, sums2.astype(jnp.bfloat16)], axis=1)
+    spread, late, back1 = lax.optimization_barrier((spread, late, back1))
+    mine = jnp.sum(exchange(spread), axis=0, dtype=jnp.float32).astype(jnp.bfloat16)
+    lowrank_all = exchange(jnp.broadcast_to(mine[None], (device_total, rank, BLOCK)))
+    late, lowrank_all = lax.optimization_barrier((late, lowrank_all))
+    back2 = exchange(late)
+    ups = pl.pallas_call(
+        rank_kernel,
+        out_shape=jax.ShapeDtypeStruct((ITEMS_DEV, rank, 2 * E), jnp.float32),
+        in_specs=[vmem] * 4,
+        out_specs=vmem,
+        compiler_params=params,
+    )(lowrank_all, packed0, packed1, packed2)
+    small = jnp.concatenate([jnp.stack([down0, down1, down2]), ups[..., :E]], axis=-1)
+    small_all = lax.all_gather(small, "seq", axis=0, tiled=True)
+    grad_qkv = pl.pallas_call(
+        unpack_kernel,
+        out_shape=jax.ShapeDtypeStruct(qkv.shape, jnp.bfloat16),
+        in_specs=[vmem] * 2,
+        out_specs=vmem,
+        compiler_params=params,
+    )(back1, back2)
+    grad_down = small_all[..., :rank].reshape(H * E, rank)
+    grad_up = jnp.swapaxes(small_all[..., rank:], 0, 1).reshape(rank, H * E)
+    return (grad_qkv, grad_down, grad_up)
+
+
+def shards(qkv, *others):
+    if ITEMS_DEV * lax.axis_size("seq") == H and qkv.shape[0] == BLOCK:
+        return whole_heads(qkv, *others)
+    return segmented(qkv, *others)
+
+
 def solution(mesh):
     return jax.shard_map(
         shards,

time: 718 us -> 246 us (0.34); the launches traced: 707 us -> 245 us
  local copies, waits for them, and re-layouts: 252 us -> 21.5 us
  other arithmetic: 182 us -> 5.22 us
  matrix products: 93.7 us -> 0 us
  waiting for transfers between devices: 121 us -> 34.1 us
  Pallas kernels: 0 us -> 80.1 us
  blocking collectives: 0 us -> 61.5 us
  starting transfers between devices: 43.2 us -> 27.9 us
    scatter-add x6 -> x0, other arithmetic: 109 us -> none  [the longest x3 54.6 us: shards(): value_sums.at[slot_now, item_blocks]]
    psum x1 -> x0, waiting for transfers between devices: 101 us -> none  [shards(): grad_down, grad_up = lax.psum((down_term, up_term), 'seq')]
    reshape x22 -> x2, local copies, waits for them, and re-layouts: 100 us -> 1.43 us  [the longest x1 1.32 us: whole_heads(): grad_up = jnp.swapaxes(small_all[..., rank:], 0, 1).reshape(rank, H * E)]
    dot_general x22 -> x0, matrix products: 93.7 us -> none  [the longest x3 27.8 us: shards(): jnp.einsum('qrk,qke->qre', weights, gathered[..., E:], preferred_element_...]
    pallas_call x0 -> x7, Pallas kernels: none -> 80.1 us  [the longest x4 73.5 us: head_pass(): pl.pallas_call(functools.partial(head_kernel, forward, backward, unfold),...]
    all_to_all x0 -> x3, blocking collectives: none -> 61.5 us  [exchange(): return lax.all_to_all(array, 'seq', 0, 0, tiled=True)]
    gather x16 -> x0, local copies, waits for them, and re-layouts: 39.8 us -> none  [the longest x3 23.5 us: shards(): jnp.take(keyval_item, item_blocks, axis=0).reshape(-1, KB * BLOCK, 2 * E)]
    all_to_all x4 -> x0, other arithmetic: 22.3 us -> none  [the longest x2 12.1 us: shards(): lax.all_to_all(spread_rows(attention_output_gradient, targets), 'seq', sp...]
  transfers between devices with their start and end apart: 7 -> 5, of which waited for: 4 -> 2; matrix products, arithmetic and copies ran while one was open for 53% -> 2% of each run, Pallas kernels for 0% -> 31%
where the time goes in v2:
time: 246 us; the launch traced here: 245 us
  Pallas kernels  80.1 us (33%)
  blocking collectives  61.5 us (25%)
  waiting for transfers between devices  34.1 us (14%)
  starting transfers between devices  27.9 us (11%)
  local copies, waits for them, and re-layouts  21.5 us (9%)
  between operations  14.3 us (6%)
  other arithmetic  5.22 us (2%)
    pallas_call x4, Pallas kernels, head_pass(): pl.pallas_call(functools.partial(head_kernel, forward, backward, unfold),...  73.5 us
    all_to_all x3, blocking collectives, exchange(): return lax.all_to_all(array, 'seq', 0, 0, tiled=True)  61.5 us
    all_to_all x4, starting transfers between devices, exchange(): return lax.all_to_all(array, 'seq', 0, 0, tiled=True)  27.8 us
    all_to_all x4, waiting for transfers between devices, exchange(): return lax.all_to_all(array, 'seq', 0, 0, tiled=True)  26.2 us
    unnamed x45, local copies, waits for them, and re-layouts  15.6 us
    all_gather x1, waiting for transfers between devices, whole_heads(): small_all = lax.all_gather(small, 'seq', axis=0, tiled=True)  7.92 us
  transfers between devices with their start and end apart: 5, of which 2 were waited for; matrix products, arithmetic and copies ran while one was open for 2% of the time, Pallas kernels for 31%

profile of v2, /device:TPU:0, one launch (start us, length us, event | category | flops | bytes accessed | tf_op | source)
XLA Modules:
  0.0 244.7 jit_solution(11972711227096651561)
XLA Ops:
  7.2 1.7 copy-done.3
  8.9 1.1 copy-done.6
  10.0 1.0 copy-done.7
  11.0 2.5 %shard_map.85 = (bf16[16,160,256]{2,1,0:T(8,128)(2,1)}, bf16[16,128,256]{2,1,0:T(8,128)(2,1)S(1)}, bf16[16,128,256]{2,1,0:T(8,128)(2,1)S(1)}) custom-call(bf16[128,9216]{1,0:T(8,128)(2,1)S(1)} %copy-done.3, bf16[128,3072]{1,0:T(8,128)(2,1)S(1)} %copy-done.6, bf16[64,3072]{1,0:T(8,128)(2,1)S(1)} %copy-done.7), custom_call_target="tpu_custom_call" | custom-call | tf_op jit(solution)/shard_map/pallas_call | solution.py:511
  13.5 1.0 copy-done.4
  14.5 1.0 copy-done.5
  15.5 7.5 %all-to-all-start = ((bf16[16,160,256]{2,1,0:T(8,128)(2,1)}), bf16[16,160,256]{2,1,0:T(8,128)(2,1)S(1)}, u32[]{:S(2)}, u32[]{:S(2)}) async-start(bf16[16,160,256]{2,1,0:T(8,128)(2,1)} %get-tuple-element.33), calls=%async_computation | async-start | bytes 2621440 | tf_op jit(solution)/shard_map/all_to_all | solution.py:509
  23.1 0.1 constant_dynamic-slice_fusion.2
  23.2 0.1 copy.26
  23.3 0.1 copy.19
  23.4 0.1 constant_dynamic-slice_fusion
  23.6 0.2 copy.25
  23.8 0.2 copy.24
  24.0 0.2 copy.27
  24.2 26.2 %all-to-all-done.refs_2_.first_ref = bf16[16,160,256]{2,1,0:T(8,128)(2,1)S(1)} async-done(((bf16[16,160,256]{2,1,0:T(8,128)(2,1)}), bf16[16,160,256]{2,1,0:T(8,128)(2,1)S(1)}, u32[]{:S(2)}, u32[]{:S(2)}) %all-to-all-start) | async-done | bytes 1310752 | tf_op jit(solution)/shard_map/all_to_all | solution.py:509
  50.4 8.0 %all-to-all-start.1 = ((bf16[16,128,256]{2,1,0:T(8,128)(2,1)}), bf16[16,128,256]{2,1,0:T(8,128)(2,1)S(1)}, u32[]{:S(2)}, u32[]{:S(2)}) async-start(bf16[16,128,256]{2,1,0:T(8,128)(2,1)} %copy-done.5), calls=%async_computation.1 | async-start | bytes 2097152 | tf_op jit(solution)/shard_map/all_to_all | solution.py:509
  58.4 0.6 fusion.6
  59.1 20.3 %shard_map.86 = (bf16[16,128,128]{2,1,0:T(8,128)(2,1)S(1)}, f32[16,128,128]{2,1,0:T(8,128)S(1)}, bf16[2048,64]{1,0:T(8,128)(2,1)S(1)}, f32[64,64]{1,0:T(8,128)S(1)}, f32[64,2048]{1,0:T(8,128)S(1)}) custom-call(s32[16,10]{1,0:T(8,128)S(1)} %bitcast.44, s32[1]{0:T(128)} %get-tuple-element.83.refs_1_, bf16[16,160,256]{2,1,0:T(8,128)(2,1)S(1)} %all-to-all-done.refs_2_.first_ref, ...), custom_call_target="tpu_custom_call" | custom-call | flops 20000000000 | bytes 4000000 | tf_op jit(solution)/shard_map/pallas_call | solution.py:439
  79.4 1.0 copy-done.8
  80.4 0.8 copy-done.10
  81.2 0.8 copy-done.16
  82.0 6.3 %all-to-all-start.2 = ((bf16[16,128,256]{2,1,0:T(8,128)(2,1)}), bf16[16,128,256]{2,1,0:T(8,128)(2,1)}, u32[]{:S(2)}, u32[]{:S(2)}) async-start(bf16[16,128,256]{2,1,0:T(8,128)(2,1)} %copy-done.4), calls=%async_computation.2 | async-start | bytes 2097152 | tf_op jit(solution)/shard_map/all_to_all | solution.py:509
  88.3 1.0 copy-done.11
  89.4 1.0 copy-done.17
  90.4 19.4 %shard_map.87 = (bf16[16,128,128]{2,1,0:T(8,128)(2,1)S(1)}, f32[16,128,128]{2,1,0:T(8,128)S(1)}, f32[64,64]{1,0:T(8,128)S(1)}, f32[64,2048]{1,0:T(8,128)S(1)}) custom-call(s32[16,10]{1,0:T(8,128)S(1)} %bitcast.43, s32[1]{0:T(128)} %get-tuple-element.84.refs_1_, bf16[16,128,256]{2,1,0:T(8,128)(2,1)S(1)} %all-to-all-done.1.refs_2_.second_ref, ...), custom_call_target="tpu_custom_call" | custom-call | flops 20000000000 | bytes 4000000 | tf_op jit(solution)/shard_map/pallas_call | solution.py:439
  109.8 0.2 fusion
  110.0 0.6 copy-done.14
  110.6 1.6 maximum_maximum_fusion
  112.2 6.0 %all-to-all-start.3 = ((bf16[16,3,128,128]{3,2,1,0:T(8,128)(2,1)}), bf16[16,3,128,128]{3,2,1,0:T(8,128)(2,1)S(1)}, u32[]{:S(2)}, u32[]{:S(2)}) async-start(bf16[16,3,128,128]{3,2,1,0:T(8,128)(2,1)} %maximum_maximum_fusion), calls=%async_computation.3 | async-start | bytes 3145728 | tf_op jit(solution)/shard_map/all_to_all | solution.py:509
  118.2 1.0 copy-done.12
  119.3 19.6 %shard_map.89 = (bf16[16,128,128]{2,1,0:T(8,128)(2,1)S(1)}, f32[16,128,128]{2,1,0:T(8,128)S(1)}) custom-call(s32[16,10]{1,0:T(8,128)S(1)} %bitcast.41, s32[1]{0:T(128)} %get-tuple-element.85.refs_1_, bf16[16,128,256]{2,1,0:T(8,128)(2,1)} %all-to-all-done.2.refs_2_.third_ref, bf16[64,128]{1,0:T(8,128)(2,1)S(1)} %get-tuple-element.80.refs_3_, ...), custom_call_target="tpu_custom_call" | custom-call | flops 20000000000 | bytes 4000000 | tf_op jit(solution)/shard_map/pallas_call | solution.py:439
  139.0 1.1 pad_maximum_fusion
  140.1 0.2 copy-done.15
  140.3 14.1 %shard_map.88 = (f32[64,64]{1,0:T(8,128)S(1)}, f32[64,2048]{1,0:T(8,128)S(1)}) custom-call(s32[16,10]{1,0:T(8,128)S(1)} %bitcast.42, s32[1]{0:T(128)} %get-tuple-element.85.refs_1_, bf16[16,128,256]{2,1,0:T(8,128)(2,1)} %all-to-all-done.2.refs_2_.third_ref, bf16[64,128]{1,0:T(8,128)(2,1)S(1)} %get-tuple-element.80.refs_3_, ...), custom_call_target="tpu_custom_call" | custom-call | flops 8000000000 | bytes 4000000 | tf_op jit(solution)/shard_map/pallas_call | solution.py:439
  154.5 0.8 bitcast_bitcast_fusion
  155.2 16.2 %all_to_all.35 = bf16[16,64,128]{2,1,0:T(8,128)(2,1)} all-to-all(bf16[16,64,128]{2,1,0:T(8,128)(2,1)} %bitcast_bitcast_fusion), channel_id=1, replica_groups=mesh['groups'=2,'seq'=16] {'seq'}, dimensions={0} | all-to-all | bytes 524288 | tf_op jit(solution)/shard_map/all_to_all | solution.py:509
  171.4 1.0 reduce_sum.12
  172.4 12.8 %all_to_all.36.lowrank_ref = bf16[16,64,128]{2,1,0:T(8,128)(2,1)S(1)} all-to-all(bf16[16,64,128]{2,1,0:T(8,128)(2,1)S(1)} %broadcast_in_dim.2), channel_id=1, replica_groups=mesh['groups'=2,'seq'=16] {'seq'}, dimensions={0} | all-to-all | bytes 524288 | tf_op jit(solution)/shard_map/all_to_all | solution.py:509
  185.3 1.2 copy-done.2
  186.5 1.8 shard_map.91
  188.2 0.7 pad_maximum_fusion.1
  189.0 32.5 %all_to_all.37.late_ref = bf16[16,2,128,128]{3,2,1,0:T(8,128)(2,1)S(1)} all-to-all(bf16[16,2,128,128]{3,2,1,0:T(8,128)(2,1)} %pad_maximum_fusion), channel_id=1, replica_groups=mesh['groups'=2,'seq'=16] {'seq'}, dimensions={0} | all-to-all | bytes 2097152 | tf_op jit(solution)/shard_map/all_to_all | solution.py:509
  221.5 2.4 shard_map.90
  223.9 7.9 %all-gather.2.cloned.1.call-done = f32[48,64,128]{2,1,0:T(8,128)} async-done(((f32[3,64,128]{2,1,0:T(8,128)}), f32[48,64,128]{2,1,0:T(8,128)}) %all-gather.2.cloned.1.call-update) | async-done | bytes 1572880 | tf_op jit(solution)/shard_map/all_gather | solution.py:569
  231.8 2.4 slice_bitcast_fusion
  234.2 0.9 copy.21
  235.2 1.3 reshape.59
  236.5 1.3 copy.22
  (36 shorter events, 0.4 us)
Async XLA Ops:
  7.2 15.9 %copy-start = (bf16[3072,64]{0,1:T(8,128)(2,1)S(1)}, bf16[3072,64]{0,1:T(8,128)(2,1)}, u32[]{:S(2)}) copy-start(bf16[3072,64]{0,1:T(8,128)(2,1)} %param.8) | copy-start | bytes 1179652
  7.2 1.7 copy-start.3
  8.9 1.1 copy-start.6
  10.0 1.0 copy-start.7
  13.5 1.0 copy-start.4
  14.5 1.0 copy-start.5
  15.5 7.5 %copy-start.19 = (s32[48]{0:T(128)S(1)}, s32[48]{0:T(128)}, u32[]{:S(2)}) copy-start(s32[48]{0:T(128)} %param.11) | copy-start | bytes 580
  15.5 7.9 %copy-start.18 = (s32[48,16,10]{0,1,2:T(8,128)S(1)}, s32[48,16,10]{0,1,2:T(8,128)}, u32[]{:S(2)}) copy-start(s32[48,16,10]{0,1,2:T(8,128)} %param.10) | copy-start | bytes 92164
  15.5 34.9 %all-to-all-start = ((bf16[16,160,256]{2,1,0:T(8,128)(2,1)}), bf16[16,160,256]{2,1,0:T(8,128)(2,1)S(1)}, u32[]{:S(2)}, u32[]{:S(2)}) async-start(bf16[16,160,256]{2,1,0:T(8,128)(2,1)} %get-tuple-element.33), calls=%async_computation | async-start | bytes 2621440 | tf_op jit(solution)/shard_map/all_to_all | solution.py:509
  50.4 31.6 %all-to-all-start.1 = ((bf16[16,128,256]{2,1,0:T(8,128)(2,1)}), bf16[16,128,256]{2,1,0:T(8,128)(2,1)S(1)}, u32[]{:S(2)}, u32[]{:S(2)}) async-start(bf16[16,128,256]{2,1,0:T(8,128)(2,1)} %copy-done.5), calls=%async_computation.1 | async-start | bytes 2097152 | tf_op jit(solution)/shard_map/all_to_all | solution.py:509
  79.4 1.0 copy-start.8
  80.4 0.8 copy-start.10
  81.2 0.8 copy-start.16
  82.0 27.8 %copy-start.1 = (bf16[16,128,256]{2,1,0:T(8,128)(2,1)}, bf16[16,128,256]{2,1,0:T(8,128)(2,1)S(1)}, u32[]{:S(2)}) copy-start(bf16[16,128,256]{2,1,0:T(8,128)(2,1)S(1)} %all-to-all-done.1.refs_2_.second_ref) | copy-start | bytes 3145732
  82.0 30.2 %all-to-all-start.2 = ((bf16[16,128,256]{2,1,0:T(8,128)(2,1)}), bf16[16,128,256]{2,1,0:T(8,128)(2,1)}, u32[]{:S(2)}, u32[]{:S(2)}) async-start(bf16[16,128,256]{2,1,0:T(8,128)(2,1)} %copy-done.4), calls=%async_computation.2 | async-start | bytes 2097152 | tf_op jit(solution)/shard_map/all_to_all | solution.py:509
  88.3 1.0 copy-start.11
  89.4 1.0 copy-start.17
  90.4 19.4 %copy-start.9 = (f32[16,128,128]{2,1,0:T(8,128)S(1)}, f32[16,128,128]{2,1,0:T(8,128)}, u32[]{:S(2)}) copy-start(f32[16,128,128]{2,1,0:T(8,128)} %copy-done.8) | copy-start | bytes 3145732
  109.8 0.8 copy-start.14
  112.2 43.0 %all-to-all-start.3 = ((bf16[16,3,128,128]{3,2,1,0:T(8,128)(2,1)}), bf16[16,3,128,128]{3,2,1,0:T(8,128)(2,1)S(1)}, u32[]{:S(2)}, u32[]{:S(2)}) async-start(bf16[16,3,128,128]{3,2,1,0:T(8,128)(2,1)} %maximum_maximum_fusion), calls=%async_computation.3 | async-start | bytes 3145728 | tf_op jit(solution)/shard_map/all_to_all | solution.py:509
  118.2 113.6 %all-gather.2.cloned.1.call-start = ((), (), s32[]{:S(2)}) async-start(), calls=%async_computation.7 | async-start | bytes 1671168 | tf_op jit(solution)/shard_map/all_gather | solution.py:569
  118.2 1.0 copy-start.12
  138.9 1.2 copy-start.13
  138.9 1.4 copy-start.15
  185.3 1.2 copy-start.2
Sparse Core Ops, SparseCore 0:
  189.1 42.6 all-gather.1

commit v3 on v2

--- a/solution.py
+++ b/solution.py
@@ -456,16 +456,65 @@
     )(lists, counts, packed, wide, down, *extra)
 
 
-def rank_kernel(lowrank_ref, first_ref, second_ref, third_ref, out_ref):
-    for within, packed_ref in enumerate((first_ref, second_ref, third_ref)):
-        total = jnp.zeros((out_ref.shape[1], 2 * E), jnp.float32)
-        for block in range(packed_ref.shape[0]):
-            total += jnp.dot(
-                lowrank_ref[block],
-                packed_ref[block, :BLOCK, : 2 * E],
+def rank_kernel(
+    spread_ref, first_ref, second_ref, third_ref, out_ref,
+    landed, mine, whole, send_part, recv_part, send_sum, recv_sum,
+):
+    count = spread_ref.shape[0]
+    me = lax.axis_index("seq")
+
+    def peer(step):
+        return lax.rem(me + step, count)
+
+    barrier = pltpu.get_barrier_semaphore()
+    for step in range(1, count):
+        pl.semaphore_signal(
+            barrier, inc=1, device_id={"seq": peer(step)}, device_id_type=pl.DeviceIdType.MESH
+        )
+    pl.semaphore_wait(barrier, count - 1)
+
+    def copy(source, target, sends, receives, step):
+        return pltpu.make_async_remote_copy(
+            src_ref=source,
+            dst_ref=target.at[step - 1],
+            send_sem=sends.at[step - 1],
+            recv_sem=receives.at[step - 1],
+            device_id={"seq": peer(step)},
+            device_id_type=pl.DeviceIdType.MESH,
+        )
+
+    parts = [
+        copy(spread_ref.at[peer(step)], landed, send_part, recv_part, step)
+        for step in range(1, count)
+    ]
+    for part in parts:
+        part.start()
+    total = spread_ref[me].astype(jnp.float32)
+    for step in range(1, count):
+        parts[step - 1].wait_recv()
+        total += landed[step - 1].astype(jnp.float32)
+    mine[...] = total.astype(jnp.bfloat16)
+    totals = [copy(mine, whole, send_sum, recv_sum, step) for step in range(1, count)]
+    for each in totals:
+        each.start()
+    packed_refs = (first_ref, second_ref, third_ref)
+    grads = [
+        jnp.dot(mine[...], ref[me, :BLOCK, : 2 * E], preferred_element_type=jnp.float32)
+        for ref in packed_refs
+    ]
+    for step in range(1, count):
+        totals[step - 1].wait_recv()
+        source = lax.rem(me + count - step, count)
+        for within, ref in enumerate(packed_refs):
+            grads[within] += jnp.dot(
+                whole[step - 1],
+                ref[source, :BLOCK, : 2 * E],
                 preferred_element_type=jnp.float32,
             )
-        out_ref[within] = total * (packed_ref.shape[0] * BLOCK) ** (-0.5)
+    for within in range(ITEMS_DEV):
+        out_ref[within] = grads[within] * (count * BLOCK) ** (-0.5)
+    for each in parts + totals:
+        each.wait_send()
 
 
 def unpack_kernel(early_ref, late_ref, out_ref):
@@ -554,17 +603,23 @@
     )
     late = jnp.stack([rows2, sums2.astype(jnp.bfloat16)], axis=1)
     spread, late, back1 = lax.optimization_barrier((spread, late, back1))
-    mine = jnp.sum(exchange(spread), axis=0, dtype=jnp.float32).astype(jnp.bfloat16)
-    lowrank_all = exchange(jnp.broadcast_to(mine[None], (device_total, rank, BLOCK)))
-    late, lowrank_all = lax.optimization_barrier((late, lowrank_all))
-    back2 = exchange(late)
     ups = pl.pallas_call(
         rank_kernel,
         out_shape=jax.ShapeDtypeStruct((ITEMS_DEV, rank, 2 * E), jnp.float32),
         in_specs=[vmem] * 4,
         out_specs=vmem,
-        compiler_params=params,
-    )(lowrank_all, packed0, packed1, packed2)
+        scratch_shapes=[
+            pltpu.VMEM((device_total - 1, rank, BLOCK), jnp.bfloat16),
+            pltpu.VMEM((rank, BLOCK), jnp.bfloat16),
+            pltpu.VMEM((device_total - 1, rank, BLOCK), jnp.bfloat16),
+        ]
+        + [pltpu.SemaphoreType.DMA((device_total - 1,))] * 4,
+        compiler_params=pltpu.CompilerParams(
+            vmem_limit_bytes=40 * 1024 * 1024, collective_id=0, has_side_effects=True
+        ),
+    )(spread, packed0, packed1, packed2)
+    late, ups = lax.optimization_barrier((late, ups))
+    back2 = exchange(late)
     small = jnp.concatenate([jnp.stack([down0, down1, down2]), ups[..., :E]], axis=-1)
     small_all = lax.all_gather(small, "seq", axis=0, tiled=True)
     grad_qkv = pl.pallas_call(

time: 246 us -> 240 us (0.976)
  blocking collectives: 61.5 us -> 33.8 us
  Pallas kernels: 80.1 us -> 98.1 us
  local copies, waits for them, and re-layouts: 21.5 us -> 25.3 us
    all_to_all x3 -> x1, blocking collectives: 61.5 us -> 33.8 us  [exchange(): return lax.all_to_all(array, 'seq', 0, 0, tiled=True)]
    pallas_call x1, Pallas kernels: 1.76 us -> 19.6 us  [whole_heads(): pl.pallas_call(rank_kernel, out_shape=jax.ShapeDtypeStruct((ITEMS_DEV, ra...]
    unnamed x45 -> x57, local copies, waits for them, and re-layouts: 15.6 us -> 18.2 us
  transfers between devices with their start and end apart: 5 -> 5, of which waited for: 2 -> 2; matrix products, arithmetic and copies ran while one was open for 2% -> 2% of each run, Pallas kernels for 31% -> 32%
where the time goes in v3:
time: 240 us; the launch traced here: 239 us
  Pallas kernels  98.1 us (41%)
  waiting for transfers between devices  36 us (15%)
  blocking collectives  33.8 us (14%)
  starting transfers between devices  27.8 us (12%)
  local copies, waits for them, and re-layouts  25.3 us (11%)
  between operations  14.3 us (6%)
  other arithmetic  3.5 us (1%)
    pallas_call x4, Pallas kernels, head_pass(): pl.pallas_call(functools.partial(head_kernel, forward, backward, unfold),...  73.6 us
    all_to_all x1, blocking collectives, exchange(): return lax.all_to_all(array, 'seq', 0, 0, tiled=True)  33.8 us
    all_to_all x4, starting transfers between devices, exchange(): return lax.all_to_all(array, 'seq', 0, 0, tiled=True)  27.6 us
    all_to_all x4, waiting for transfers between devices, exchange(): return lax.all_to_all(array, 'seq', 0, 0, tiled=True)  26.2 us
    pallas_call x1, Pallas kernels, whole_heads(): pl.pallas_call(rank_kernel, out_shape=jax.ShapeDtypeStruct((ITEMS_DEV, ra...  19.6 us
    unnamed x57, local copies, waits for them, and re-layouts  18.2 us
    all_gather x1, waiting for transfers between devices, whole_heads(): small_all = lax.all_gather(small, 'seq', axis=0, tiled=True)  9.75 us
  transfers between devices with their start and end apart: 5, of which 2 were waited for; matrix products, arithmetic and copies ran while one was open for 2% of the time, Pallas kernels for 32%

profile of v3, /device:TPU:0, one launch (start us, length us, event | category | flops | bytes accessed | tf_op | source)
XLA Modules:
  0.0 238.9 jit_solution(15302969629273042790)
XLA Ops:
  7.2 1.7 copy-done.3
  8.9 1.1 copy-done.6
  10.0 1.0 copy-done.7
  11.0 2.5 %shard_map.85 = (bf16[16,160,256]{2,1,0:T(8,128)(2,1)}, bf16[16,128,256]{2,1,0:T(8,128)(2,1)S(1)}, bf16[16,128,256]{2,1,0:T(8,128)(2,1)S(1)}) custom-call(bf16[128,9216]{1,0:T(8,128)(2,1)S(1)} %copy-done.3, bf16[128,3072]{1,0:T(8,128)(2,1)S(1)} %copy-done.6, bf16[64,3072]{1,0:T(8,128)(2,1)S(1)} %copy-done.7), custom_call_target="tpu_custom_call" | custom-call | tf_op jit(solution)/shard_map/pallas_call | solution.py:560
  13.5 1.0 copy-done.4
  14.5 1.0 copy-done.5
  15.5 7.5 %all-to-all-start = ((bf16[16,160,256]{2,1,0:T(8,128)(2,1)}), bf16[16,160,256]{2,1,0:T(8,128)(2,1)S(1)}, u32[]{:S(2)}, u32[]{:S(2)}) async-start(bf16[16,160,256]{2,1,0:T(8,128)(2,1)} %get-tuple-element.33), calls=%async_computation | async-start | bytes 2621440 | tf_op jit(solution)/shard_map/all_to_all | solution.py:558
  23.1 0.1 constant_dynamic-slice_fusion.2
  23.2 0.1 copy.27
  23.3 0.1 copy.20
  23.5 0.1 constant_dynamic-slice_fusion
  23.6 0.2 copy.26
  23.8 0.2 copy.25
  24.0 0.2 copy.28
  24.3 26.2 %all-to-all-done.refs_2_.first_ref = bf16[16,160,256]{2,1,0:T(8,128)(2,1)S(1)} async-done(((bf16[16,160,256]{2,1,0:T(8,128)(2,1)}), bf16[16,160,256]{2,1,0:T(8,128)(2,1)S(1)}, u32[]{:S(2)}, u32[]{:S(2)}) %all-to-all-start) | async-done | bytes 1310752 | tf_op jit(solution)/shard_map/all_to_all | solution.py:558
  50.5 8.0 %all-to-all-start.1 = ((bf16[16,128,256]{2,1,0:T(8,128)(2,1)}), bf16[16,128,256]{2,1,0:T(8,128)(2,1)S(1)}, u32[]{:S(2)}, u32[]{:S(2)}) async-start(bf16[16,128,256]{2,1,0:T(8,128)(2,1)} %copy-done.5), calls=%async_computation.1 | async-start | bytes 2097152 | tf_op jit(solution)/shard_map/all_to_all | solution.py:558
  58.5 0.7 fusion.6
  59.1 20.3 %shard_map.86 = (bf16[16,128,128]{2,1,0:T(8,128)(2,1)S(1)}, f32[16,128,128]{2,1,0:T(8,128)S(1)}, bf16[2048,64]{1,0:T(8,128)(2,1)S(1)}, f32[64,64]{1,0:T(8,128)S(1)}, f32[64,2048]{1,0:T(8,128)S(1)}) custom-call(s32[16,10]{1,0:T(8,128)S(1)} %bitcast.44, s32[1]{0:T(128)} %get-tuple-element.83.refs_1_, bf16[16,160,256]{2,1,0:T(8,128)(2,1)S(1)} %all-to-all-done.refs_2_.first_ref, ...), custom_call_target="tpu_custom_call" | custom-call | flops 20000000000 | bytes 4000000 | tf_op jit(solution)/shard_map/pallas_call | solution.py:439
  79.5 1.0 copy-done.8
  80.5 0.6 copy-done.10
  81.1 0.8 copy-done.16
  81.9 0.8 copy-done.22
  82.6 6.1 %all-to-all-start.2 = ((bf16[16,128,256]{2,1,0:T(8,128)(2,1)}), bf16[16,128,256]{2,1,0:T(8,128)(2,1)}, u32[]{:S(2)}, u32[]{:S(2)}) async-start(bf16[16,128,256]{2,1,0:T(8,128)(2,1)} %copy-done.4), calls=%async_computation.2 | async-start | bytes 2097152 | tf_op jit(solution)/shard_map/all_to_all | solution.py:558
  88.7 1.0 copy-done.17
  89.8 1.0 copy-done.23
  90.8 19.4 %shard_map.87 = (bf16[16,128,128]{2,1,0:T(8,128)(2,1)S(1)}, f32[16,128,128]{2,1,0:T(8,128)S(1)}, f32[64,64]{1,0:T(8,128)S(1)}, f32[64,2048]{1,0:T(8,128)S(1)}) custom-call(s32[16,10]{1,0:T(8,128)S(1)} %bitcast.43, s32[1]{0:T(128)} %get-tuple-element.84.refs_1_, bf16[16,128,256]{2,1,0:T(8,128)(2,1)S(1)} %all-to-all-done.1.refs_2_.second_ref, ...), custom_call_target="tpu_custom_call" | custom-call | flops 20000000000 | bytes 4000000 | tf_op jit(solution)/shard_map/pallas_call | solution.py:439
  110.2 0.2 fusion
  110.4 0.4 copy-done.12
  110.8 0.2 copy-done.20
  111.0 1.5 maximum_maximum_fusion
  112.6 6.0 %all-to-all-start.3 = ((bf16[16,3,128,128]{3,2,1,0:T(8,128)(2,1)}), bf16[16,3,128,128]{3,2,1,0:T(8,128)(2,1)S(1)}, u32[]{:S(2)}, u32[]{:S(2)}) async-start(bf16[16,3,128,128]{3,2,1,0:T(8,128)(2,1)} %maximum_maximum_fusion), calls=%async_computation.3 | async-start | bytes 3145728 | tf_op jit(solution)/shard_map/all_to_all | solution.py:558
  118.6 0.2 all-gather.2.cloned.1.call-start
  118.8 1.0 copy-done.18
  119.9 19.7 %shard_map.89 = (bf16[16,128,128]{2,1,0:T(8,128)(2,1)S(1)}, f32[16,128,128]{2,1,0:T(8,128)S(1)}) custom-call(s32[16,10]{1,0:T(8,128)S(1)} %bitcast.41, s32[1]{0:T(128)} %get-tuple-element.85.refs_1_, bf16[16,128,256]{2,1,0:T(8,128)(2,1)} %all-to-all-done.2.refs_2_.third_ref, bf16[64,128]{1,0:T(8,128)(2,1)S(1)} %get-tuple-element.80.refs_3_, ...), custom_call_target="tpu_custom_call" | custom-call | flops 20000000000 | bytes 4000000 | tf_op jit(solution)/shard_map/pallas_call | solution.py:439
  139.7 1.1 pad_maximum_fusion
  140.8 0.2 copy-done.21
  141.0 14.2 %shard_map.88 = (f32[64,64]{1,0:T(8,128)S(1)}, f32[64,2048]{1,0:T(8,128)S(1)}) custom-call(s32[16,10]{1,0:T(8,128)S(1)} %bitcast.42, s32[1]{0:T(128)} %get-tuple-element.85.refs_1_, bf16[16,128,256]{2,1,0:T(8,128)(2,1)} %all-to-all-done.2.refs_2_.third_ref, bf16[64,128]{1,0:T(8,128)(2,1)S(1)} %get-tuple-element.80.refs_3_, ...), custom_call_target="tpu_custom_call" | custom-call | flops 8000000000 | bytes 4000000 | tf_op jit(solution)/shard_map/pallas_call | solution.py:439
  155.2 0.6 copy-done.14
  155.9 1.2 copy-done.2
  157.1 19.6 %shard_map.90 = f32[3,64,128]{2,1,0:T(8,128)S(1)} custom-call(bf16[16,64,128]{2,1,0:T(8,128)(2,1)S(1)} %bitcast_bitcast_fusion.spread_ref, bf16[16,160,256]{2,1,0:T(8,128)(2,1)S(1)} %all-to-all-done.refs_2_.first_ref, bf16[16,128,256]{2,1,0:T(8,128)(2,1)S(1)} %copy-done.2, bf16[16,128,256]{2,1,0:T(8,128)(2,1)} %all-to-all-done.2.refs_2_.third_ref), custom_call_target="tpu_custom_call" | custom-call | tf_op jit(solution)/shard_map/pallas_call | solution.py:606
  176.7 0.7 pad_maximum_fusion.1
  177.5 33.8 %all_to_all.25.late_ref = bf16[16,2,128,128]{3,2,1,0:T(8,128)(2,1)S(1)} all-to-all(bf16[16,2,128,128]{3,2,1,0:T(8,128)(2,1)} %pad_maximum_fusion), channel_id=1, replica_groups=mesh['groups'=2,'seq'=16] {'seq'}, dimensions={0} | all-to-all | bytes 2097152 | tf_op jit(solution)/shard_map/all_to_all | solution.py:558
  211.3 2.3 shard_map.91
  213.7 9.8 %all-gather.2.cloned.1.call-done = f32[48,64,128]{2,1,0:T(8,128)} async-done(((f32[3,64,128]{2,1,0:T(8,128)}), f32[48,64,128]{2,1,0:T(8,128)}) %all-gather.2.cloned.1.call-update) | async-done | bytes 1572880 | tf_op jit(solution)/shard_map/all_gather | solution.py:624
  223.4 3.6 %slice_bitcast_fusion = (f32[64,48,64]{2,0,1:T(8,128)S(1)}, f32[48,64,64]{2,1,0:T(8,128)}) fusion(f32[48,64,128]{2,1,0:T(8,128)} %all-gather.2.cloned.1.call-done), kind=kLoop, calls=%fused_computation | loop fusion | bytes 3145728 | tf_op jit(solution)/shard_map/transpose | solution.py:633
  227.1 0.9 copy.22
  228.0 1.3 reshape.58
  229.3 2.7 %copy.23 = f32[3072,64]{0,1:T(8,128)} copy(f32[3072,64]{1,0:T(8,128)} %bitcast.45) | data formatting | bytes 1572864
  (44 shorter events, 0.3 us)
Async XLA Ops:
  7.2 16.0 %copy-start = (bf16[3072,64]{0,1:T(8,128)(2,1)S(1)}, bf16[3072,64]{0,1:T(8,128)(2,1)}, u32[]{:S(2)}) copy-start(bf16[3072,64]{0,1:T(8,128)(2,1)} %param.8) | copy-start | bytes 1179652
  7.2 1.7 copy-start.3
  8.9 1.1 copy-start.6
  10.0 1.0 copy-start.7
  13.5 1.0 copy-start.4
  14.5 1.0 copy-start.5
  15.5 7.5 %copy-start.25 = (s32[48]{0:T(128)S(1)}, s32[48]{0:T(128)}, u32[]{:S(2)}) copy-start(s32[48]{0:T(128)} %param.11) | copy-start | bytes 580
  15.5 7.9 %copy-start.24 = (s32[48,16,10]{0,1,2:T(8,128)S(1)}, s32[48,16,10]{0,1,2:T(8,128)}, u32[]{:S(2)}) copy-start(s32[48,16,10]{0,1,2:T(8,128)} %param.10) | copy-start | bytes 92164
  15.5 34.9 %all-to-all-start = ((bf16[16,160,256]{2,1,0:T(8,128)(2,1)}), bf16[16,160,256]{2,1,0:T(8,128)(2,1)S(1)}, u32[]{:S(2)}, u32[]{:S(2)}) async-start(bf16[16,160,256]{2,1,0:T(8,128)(2,1)} %get-tuple-element.33), calls=%async_computation | async-start | bytes 2621440 | tf_op jit(solution)/shard_map/all_to_all | solution.py:558
  50.5 32.2 %all-to-all-start.1 = ((bf16[16,128,256]{2,1,0:T(8,128)(2,1)}), bf16[16,128,256]{2,1,0:T(8,128)(2,1)S(1)}, u32[]{:S(2)}, u32[]{:S(2)}) async-start(bf16[16,128,256]{2,1,0:T(8,128)(2,1)} %copy-done.5), calls=%async_computation.1 | async-start | bytes 2097152 | tf_op jit(solution)/shard_map/all_to_all | solution.py:558
  79.5 1.0 copy-start.8
  80.5 0.6 copy-start.10
  81.1 0.8 copy-start.16
  81.8 0.8 copy-start.22
  82.6 27.6 %copy-start.1 = (bf16[16,128,256]{2,1,0:T(8,128)(2,1)}, bf16[16,128,256]{2,1,0:T(8,128)(2,1)S(1)}, u32[]{:S(2)}) copy-start(bf16[16,128,256]{2,1,0:T(8,128)(2,1)S(1)} %all-to-all-done.1.refs_2_.second_ref) | copy-start | bytes 3145732
  82.6 29.9 %all-to-all-start.2 = ((bf16[16,128,256]{2,1,0:T(8,128)(2,1)}), bf16[16,128,256]{2,1,0:T(8,128)(2,1)}, u32[]{:S(2)}, u32[]{:S(2)}) async-start(bf16[16,128,256]{2,1,0:T(8,128)(2,1)} %copy-done.4), calls=%async_computation.2 | async-start | bytes 2097152 | tf_op jit(solution)/shard_map/all_to_all | solution.py:558
  88.7 1.0 copy-start.17
  89.8 1.0 copy-start.23
  90.8 19.4 %copy-start.9 = (f32[16,128,128]{2,1,0:T(8,128)S(1)}, f32[16,128,128]{2,1,0:T(8,128)}, u32[]{:S(2)}) copy-start(f32[16,128,128]{2,1,0:T(8,128)} %copy-done.8) | copy-start | bytes 3145732
  110.2 0.6 copy-start.12
  110.2 0.8 copy-start.20
  112.6 43.3 %all-to-all-start.3 = ((bf16[16,3,128,128]{3,2,1,0:T(8,128)(2,1)}), bf16[16,3,128,128]{3,2,1,0:T(8,128)(2,1)S(1)}, u32[]{:S(2)}, u32[]{:S(2)}) async-start(bf16[16,3,128,128]{3,2,1,0:T(8,128)(2,1)} %maximum_maximum_fusion), calls=%async_computation.3 | async-start | bytes 3145728 | tf_op jit(solution)/shard_map/all_to_all | solution.py:558
  118.6 104.8 %all-gather.2.cloned.1.call-start = ((), (), s32[]{:S(2)}) async-start(), calls=%async_computation.5 | async-start | bytes 1671168 | tf_op jit(solution)/shard_map/all_gather | solution.py:624
  118.8 1.0 copy-start.18
  139.6 1.2 copy-start.19
  139.6 1.4 copy-start.21
  155.2 0.6 copy-start.14
  155.9 1.2 copy-start.2
  157.1 19.6 %copy-start.11 = (f32[64,64]{1,0:T(8,128)S(1)}, f32[64,64]{1,0:T(8,128)}, u32[]{:S(2)}) copy-start(f32[64,64]{1,0:T(8,128)} %copy-done.10) | copy-start | bytes 49156
  157.1 19.6 %copy-start.13 = (f32[64,64]{1,0:T(8,128)S(1)}, f32[64,64]{1,0:T(8,128)}, u32[]{:S(2)}) copy-start(f32[64,64]{1,0:T(8,128)} %copy-done.12) | copy-start | bytes 49156
  157.1 19.6 %copy-start.15 = (f32[64,64]{1,0:T(8,128)S(1)}, f32[64,64]{1,0:T(8,128)}, u32[]{:S(2)}) copy-start(f32[64,64]{1,0:T(8,128)} %copy-done.14) | copy-start | bytes 49156
Sparse Core Ops, SparseCore 0:
  177.6 45.7 all-gather.1
